TPU v7x, 256 devices: a whole 4x4x8 slice. The times are simulated.
256 devices in a mesh: dx: 32 (over y, z), dy: 8 (over x, core).
Axes of the slice: x: 4, y: 4, z: 8, core: 2. Of those that a mesh axis runs over, the one named last changes fastest.
Arguments:
- positions: float32 [32, 8, 3, 128], P('dx', 'dy'), may hold values from 0 to 1
- velocities: float32 [32, 8, 3, 128], P('dx', 'dy'), may hold values from -3 to 3
- species: int32 [32, 8, 128], P('dx', 'dy'), may hold values from 0 to 3
- neighbours: int32 [32, 8, 16, 128], P('dx', 'dy'), may hold values from -1 to 1151, as said below
- emb: bfloat16 [4, 28], replicated, may hold values from -4 to 4
- w_in: bfloat16 [128, 64], replicated, may hold values from -0.75 to 0.75
- w_two: bfloat16 [64, 128], replicated, may hold values from -0.5 to 0.5
- w_val: bfloat16 [192, 64], replicated, may hold values from -0.75 to 0.75
- w_env: bfloat16 [192, 64], replicated, may hold values from -0.75 to 0.75
- w_mix: bfloat16 [128, 256], replicated, may hold values from -0.375 to 0.375
- w_lat: bfloat16 [64, 128], replicated, may hold values from -0.5 to 0.5
- w_out: float32 [64], replicated, may hold values from -0.75 to 0.75
Outputs:
- positions_out: float32 [32, 8, 3, 128], P('dx', 'dy')
- velocities_out: float32 [32, 8, 3, 128], P('dx', 'dy')
- forces_out: float32 [32, 8, 3, 128], P('dx', 'dy')
Inputs may be any that keep to these rules, and one draw needn't show every extreme that they name: `neighbours`: -1 marks an empty slot; every other entry is a ghost number o * 128 + a whose atom a lies in a block of domain slot o that has some entry of 0 or more, and never the slot's own centre. The blocks with any entry of 0 or more come first in each domain; every atom of such a block has at least 12 filled slots, placed first. Every domain has at least 4 such blocks and some domain has all 16.
All inputs are finite; a program needn't handle non-finite values.
Results may differ from a plain program's by a relative error of at most 0.04.
Values sent between devices are 32-bit elements; how exact they have to be, the bound alone decides.
A program may use at most 128 MiB of HBM per device.

v0:
```python
import math

import jax
import jax.numpy as jnp
from jax import lax
from jax.sharding import PartitionSpec as P

C = 64
NBASIS = 8
NS = 4
SLOTS = 16
STEPS = 2
CENTERS = 8
GROUP = 8


TIME_STEP = 0.2
CUTOFF = 4.5
SOFTEN = 0.04
MASSES = (3.0, 2.0, 1.5, 1.0)


def padded(shard, sides, width):
    for axis, dim in sides:
        count, length = (lax.axis_size(axis), shard.shape[dim])
        up = [(i, (i + 1) % count) for i in range(count)]
        down = [(j, i) for i, j in up]
        last = lax.slice_in_dim(shard, length - width, length, axis=dim)
        initial = lax.slice_in_dim(shard, 0, width, axis=dim)
        before = lax.ppermute(last, axis, up)
        after = lax.ppermute(initial, axis, down)
        shard = jnp.concatenate([before, shard, after], axis=dim)
    return shard


def matmul(left, right):
    return jnp.dot(
        left.astype(jnp.float32), right.astype(jnp.float32), preferred_element_type=jnp.float32
    )


def harmonics(unit):
    ux, uy, uz = (unit[0], unit[1], unit[2])
    root3 = math.sqrt(3.0)
    root5 = math.sqrt(5.0)
    root15 = math.sqrt(15.0)
    return jnp.stack(
        [
            jnp.ones_like(ux),
            root3 * ux,
            root3 * uy,
            root3 * uz,
            root15 * ux * uy,
            root15 * uy * uz,
            0.5 * root5 * (3.0 * uz * uz - 1.0),
            root15 * ux * uz,
            0.5 * root15 * (ux * ux - uy * uy),
        ]
    )


def spread_orders(table):
    return jnp.concatenate(
        [table[0:1], jnp.repeat(table[1:2], 3, axis=0), jnp.repeat(table[2:3], 5, axis=0)], axis=0
    )


def edge_energy(rel, valid, feats, params):
    w_in, w_two, w_val, w_env, w_mix, w_lat, w_out = params
    edges = rel.shape[1]
    dist_sq = jnp.sum(rel * rel, axis=0) + SOFTEN
    dist = jnp.sqrt(dist_sq)
    unit = rel / dist
    cut = valid * (1.0 - dist_sq / (CUTOFF * CUTOFF)) ** 2
    freq = jnp.arange(1, NBASIS + 1, dtype=jnp.float32)[:, None]
    basis = jnp.sin(freq * (math.pi / CUTOFF) * dist) / dist * cut
    sph = harmonics(unit)
    zin = jnp.concatenate([basis.astype(jnp.bfloat16), feats], axis=0)
    hidden = jax.nn.silu(matmul(w_in, zin)).astype(jnp.bfloat16)
    latent = matmul(w_two, hidden) * cut
    latent_b = latent.astype(jnp.bfloat16)
    value = matmul(w_val, latent_b).reshape(3, C, edges)
    envw = matmul(w_env, latent_b).reshape(3, C, edges)
    env = (spread_orders(envw) * sph[:, None, :]).reshape(9, C, edges // SLOTS, SLOTS).sum(
        axis=3
    ) / SLOTS
    env_rep = jnp.repeat(env, SLOTS, axis=2)
    prod = spread_orders(value) * sph[:, None, :] * env_rep
    scal = jnp.concatenate([prod[0], prod[1:4].sum(axis=0), prod[4:9].sum(axis=0)], axis=0)
    mixed = jnp.concatenate([latent, scal], axis=0).astype(jnp.bfloat16)
    hidden2 = jax.nn.silu(matmul(w_mix, mixed)).astype(jnp.bfloat16)
    final = latent + matmul(w_lat, hidden2)
    return jnp.sum(w_out[:, None] * final * cut)


def group_grads(rel4, feats, params):
    nblk = rel4.shape[1]
    width = rel4.shape[2]
    rel = rel4[:3].reshape(3, nblk * width)
    valid = rel4[3].reshape(nblk * width)
    flat_feats = feats.reshape(feats.shape[0], nblk * width)

    def compute(unused):
        return jax.grad(edge_energy)(rel, valid, flat_feats, params).reshape(3, nblk, width)

    def skipped(unused):
        return jnp.zeros((3, nblk, width), jnp.float32)

    return lax.cond(jnp.any(valid > 0.0), compute, skipped, 0)


def run_blocks(rel4, feats, params, trips):
    nblk = rel4.shape[1]
    width = rel4.shape[2]

    def one_group(step, total):
        start = step * GROUP
        rel_part = lax.dynamic_slice_in_dim(rel4, start, GROUP, 1)
        feat_part = lax.dynamic_slice_in_dim(feats, start, GROUP, 1)
        return lax.dynamic_update_slice_in_dim(
            total, group_grads(rel_part, feat_part, params), start, 1
        )

    return lax.fori_loop(0, trips, one_group, jnp.zeros((3, nblk, width), jnp.float32))


def species_lookup(emb, kinds):
    onehot = (kinds.reshape(-1)[None, :] == jnp.arange(NS, dtype=jnp.int32)[:, None]).astype(
        jnp.float32
    )
    looked = matmul(emb.T, onehot).astype(jnp.bfloat16)
    return looked.reshape((emb.shape[1],) + kinds.shape)


def build_edges(coords, ghost_kinds, place, kinds, nbrs, emb):
    nblk = nbrs.shape[0]
    valid = (nbrs >= 0).astype(jnp.float32)
    index = jnp.maximum(nbrs, 0)
    far_end = coords[:, index]
    centre = jnp.repeat(place.reshape(3, nblk, CENTERS), SLOTS, axis=2)
    rel4 = jnp.concatenate([far_end - centre, valid[None]], axis=0)
    centre_kind = jnp.repeat(kinds.reshape(nblk, CENTERS), SLOTS, axis=1)
    far_kind = ghost_kinds[index]
    feats = jnp.concatenate(
        [species_lookup(emb, centre_kind), species_lookup(emb, far_kind)], axis=0
    )
    return (rel4, feats, jnp.stack([centre_kind, far_kind]).astype(jnp.float32))


def split_terms(grads, nbrs, atoms):
    nblk = nbrs.shape[0]
    valid = (nbrs >= 0).astype(jnp.float32)
    masked = grads * valid[None]
    centre = masked.reshape(3, nblk, CENTERS, SLOTS).sum(axis=3).reshape(3, atoms)
    index = jnp.maximum(nbrs, 0).reshape(-1)
    ghost = jax.vmap(lambda comp: jax.ops.segment_sum(comp, index, num_segments=9 * atoms))(
        masked.reshape(3, -1)
    )
    return (centre, -ghost)


def per_device(
    positions, velocities, species, neighbours, emb, w_in, w_two, w_val, w_env, w_mix, w_lat, w_out
):
    params = (w_in, w_two, w_val, w_env, w_mix, w_lat, w_out)
    place = positions[0, 0]
    speed = velocities[0, 0]
    kinds = species[0, 0]
    nbrs = neighbours[0, 0]
    atoms = place.shape[1]
    live = jnp.sum(jnp.any(nbrs >= 0, axis=1).astype(jnp.int32))
    kind_row = kinds.astype(jnp.float32)[None]
    shifts = jnp.array(
        [[pidx - 1, qidx - 1, 0] for pidx in range(3) for qidx in range(3)], dtype=jnp.float32
    )
    mass = jnp.zeros(kinds.shape, jnp.float32)
    for kind in range(4):
        mass = mass + jnp.where(kinds == kind, MASSES[kind], 0.0).astype(jnp.float32)
    inv_mass = (1.0 / mass)[None, :]

    def forces_at(where_now):
        sendable = jnp.concatenate([where_now, kind_row], axis=0)[None, None]
        ext = padded(sendable, (("dx", 0), ("dy", 1)), 1)
        ext = ext.reshape(9, 4, atoms)
        coords = (ext[:, :3] + shifts[:, :, None]).transpose(1, 0, 2).reshape(3, 9 * atoms)
        gkinds = ext[:, 3].reshape(9 * atoms).astype(jnp.int32)
        rel4, feats, kind_rows = build_edges(coords, gkinds, where_now, kinds, nbrs, emb)
        grads = run_blocks(rel4, feats, params, (live + GROUP - 1) // GROUP)
        centre, ghost = split_terms(grads, nbrs, atoms)
        packed = ghost.reshape(3, 9, atoms).transpose(1, 0, 2).reshape(1, 1, 27 * atoms)
        got = padded(packed, (("dx", 0), ("dy", 1)), 1)
        got = got.reshape(3, 3, 9, 3, atoms)
        returned = jnp.zeros((3, atoms), jnp.float32)
        for pidx in range(3):
            for qidx in range(3):
                returned = returned + got[pidx, qidx, (2 - pidx) * 3 + (2 - qidx)]
        return centre + returned

    force = forces_at(place)
    for step in range(STEPS):
        speed = speed + 0.5 * TIME_STEP * inv_mass * force
        place = place + TIME_STEP * speed
        force = forces_at(place)
        speed = speed + 0.5 * TIME_STEP * inv_mass * force
    return (place[None, None], speed[None, None], force[None, None])


def solution(mesh):
    in_specs = (
        P("dx", "dy", None, None),
        P("dx", "dy", None, None),
        P("dx", "dy", None),
        P("dx", "dy", None, None),
        P(),
        P(),
        P(),
        P(),
        P(),
        P(),
        P(),
        P(),
    )
    out_specs = (P("dx", "dy", None, None), P("dx", "dy", None, None), P("dx", "dy", None, None))
    return jax.shard_map(
        per_device, mesh=mesh, in_specs=in_specs, out_specs=out_specs, check_vma=False
    )
```

profile of v0, /device:TPU:16, one launch (start us, length us, event | category | flops | bytes accessed | tf_op | source)
XLA Modules:
  0.0 588.3 jit_solution(12416585193901696962)
XLA Ops:
  3.3 5.8 collective-permute-start.1
  22.0 5.5 gather_fusion
  27.8 11.8 %gather_fusion.1 = s32[2048]{0:T(1024)S(1)} fusion(s32[1152]{0:T(1024)S(1)} %bitcast.495, s32[2048]{0:T(1024)S(1)} %broadcast_clamp_fusion), kind=kCustom, calls=%fused_computation.1 | custom fusion | bytes 24576 | tf_op jit(solution)/shard_map/gather | solution.py:143
  41.8 133.6 %while.30 = (s32[]{:T(128)}, f32[3,16,128]{2,1,0:T(8,128)}, s32[]{:T(128)}, f32[4,16,128]{2,1,0:T(8,128)}, bf16[56,16,128]{2,1,0:T(8,128)(2,1)}, /*index=5*/bf16...) while((s32[]{:T(128)}, f32[3,16,128]{2,1,0:T(8,128)}, ...), condition=%wide.region_23.24_spmd, body=%wide.region_2.23_spmd.sunk | while | flops 360825856 | bytes 144035920 | solution.py:124
  44.7 63.3 %conditional.6 = (f32[3,8,128]{2,1,0:T(8,128)S(1)}) conditional(s32[]{:T(128)} %convert_element_type.694, () %tuple.173, (f32[4,8,128]{2,1,0:T(8,128)S(1)}, f32[1,8,128]{2,1,0:T(8,128)S(1)}, bf16[56,16,128]{2,1,0:T(8,128)(2,1)}, s32[]{:T(128)}, bf16[128,64]{1,0:T(8,128)(2,1)S(1)}, /*index=5*/bf16[64,128]{1,0:T(8,128)(2,1)}, ...), branch_computations={%region_4.4_spmd, %region_5.22_spmd} | conditional | flops 360823808 | bytes 143969536 | solution.py:109
  56.6 4.5 fusion.2
  63.7 5.2 copy.40
  78.9 4.2 fusion.10
  83.1 4.9 copy.42
  88.0 3.6 bitcast_reduce_fusion
  98.1 3.8 copy.43
  111.3 63.3 %conditional.6 = (f32[3,8,128]{2,1,0:T(8,128)S(1)}) conditional(s32[]{:T(128)} %convert_element_type.694, () %tuple.173, (f32[4,8,128]{2,1,0:T(8,128)S(1)}, f32[1,8,128]{2,1,0:T(8,128)S(1)}, bf16[56,16,128]{2,1,0:T(8,128)(2,1)}, s32[]{:T(128)}, bf16[128,64]{1,0:T(8,128)(2,1)S(1)}, /*index=5*/bf16[64,128]{1,0:T(8,128)(2,1)}, ...), branch_computations={%region_4.4_spmd, %region_5.22_spmd} | conditional | flops 360823808 | bytes 143969536 | solution.py:109
  123.3 4.5 fusion.2
  130.3 5.2 copy.40
  145.5 4.2 fusion.10
  149.7 4.9 copy.42
  154.6 3.6 bitcast_reduce_fusion
  164.8 3.8 copy.43
  176.6 11.7 %scatter_custom_fusion = f32[3,1152]{0,1:T(8,128)S(1)} fusion(s32[2048]{0:T(1024)} %maximum_bitcast_fusion, f32[2048,3]{1,0:T(8,128)S(1)} %bitcast.551, f32[]{:T(128)} %constant.256.clone.1), kind=kCustom, calls=%fused_computation.512 | custom fusion | flops 6144 | bytes 14336 | tf_op jit(solution)/shard_map/vmap()/scatter-add | solution.py:156
  188.8 4.1 collective-permute-start.5
  201.9 4.0 collective-permute-start.9
  207.2 4.4 collective-permute-done.8
  216.3 5.5 gather_fusion.2
  222.7 11.8 %gather_fusion.3 = s32[2048]{0:T(1024)S(1)} fusion(s32[1152]{0:T(1024)S(1)} %bitcast.494, s32[2048]{0:T(1024)S(1)} %copy-done.101), kind=kCustom, calls=%fused_computation.3 | custom fusion | bytes 24576 | tf_op jit(solution)/shard_map/gather | solution.py:143
  236.1 134.0 %while.31 = (s32[]{:T(128)}, f32[3,16,128]{2,1,0:T(8,128)}, s32[]{:T(128)}, f32[4,16,128]{2,1,0:T(8,128)}, bf16[56,16,128]{2,1,0:T(8,128)(2,1)}, /*index=5*/bf16...) while((s32[]{:T(128)}, f32[3,16,128]{2,1,0:T(8,128)}, ...), condition=%wide.region_47.48_spmd, body=%wide.region_26.47_spmd.sunk | while | flops 360825856 | bytes 144035920 | solution.py:124
  239.3 63.3 %conditional.7 = (f32[3,8,128]{2,1,0:T(8,128)S(1)}) conditional(s32[]{:T(128)} %convert_element_type.695, () %tuple.177, (f32[4,8,128]{2,1,0:T(8,128)S(1)}, f32[1,8,128]{2,1,0:T(8,128)S(1)}, bf16[56,16,128]{2,1,0:T(8,128)(2,1)}, s32[]{:T(128)}, bf16[128,64]{1,0:T(8,128)(2,1)S(1)}, /*index=5*/bf16[64,128]{1,0:T(8,128)(2,1)}, ...), branch_computations={%region_28.28_spmd, %region_29.46_spmd} | conditional | flops 360823808 | bytes 143969536 | solution.py:109
  251.3 4.5 fusion.93
  258.3 5.2 copy.47
  273.5 4.2 fusion.101
  277.7 4.9 copy.49
  282.6 3.6 bitcast_reduce_fusion.1
  292.7 3.8 copy.50
  306.1 63.3 %conditional.7 = (f32[3,8,128]{2,1,0:T(8,128)S(1)}) conditional(s32[]{:T(128)} %convert_element_type.695, () %tuple.177, (f32[4,8,128]{2,1,0:T(8,128)S(1)}, f32[1,8,128]{2,1,0:T(8,128)S(1)}, bf16[56,16,128]{2,1,0:T(8,128)(2,1)}, s32[]{:T(128)}, bf16[128,64]{1,0:T(8,128)(2,1)S(1)}, /*index=5*/bf16[64,128]{1,0:T(8,128)(2,1)}, ...), branch_computations={%region_28.28_spmd, %region_29.46_spmd} | conditional | flops 360823808 | bytes 143969536 | solution.py:109
  318.0 4.5 fusion.93
  325.0 5.2 copy.47
  340.2 4.2 fusion.101
  344.4 4.9 copy.49
  349.3 3.6 bitcast_reduce_fusion.1
  359.4 3.8 copy.50
  371.3 11.7 %scatter_custom_fusion.1 = f32[3,1152]{0,1:T(8,128)S(1)} fusion(s32[2048]{0:T(1024)} %maximum_bitcast_fusion, f32[2048,3]{1,0:T(8,128)S(1)} %bitcast.552, f32[]{:T(128)} %constant.256.clone.1), kind=kCustom, calls=%fused_computation.510 | custom fusion | flops 6144 | bytes 14336 | tf_op jit(solution)/shard_map/vmap()/scatter-add | solution.py:156
  383.5 4.1 collective-permute-start.13
  391.0 3.0 collective-permute-done.14
  394.3 4.2 collective-permute-start.17
  399.8 4.4 collective-permute-done.16
  408.9 5.5 gather_fusion.4
  415.3 11.8 %gather_fusion.5 = s32[2048]{0:T(1024)S(1)} fusion(s32[1152]{0:T(1024)S(1)} %bitcast.493, s32[2048]{0:T(1024)S(1)} %copy-done.102), kind=kCustom, calls=%fused_computation.5 | custom fusion | bytes 24576 | tf_op jit(solution)/shard_map/gather | solution.py:143
  428.7 133.5 %while.32 = (s32[]{:T(128)}, f32[3,16,128]{2,1,0:T(8,128)}, s32[]{:T(128)}, f32[4,16,128]{2,1,0:T(8,128)}, bf16[56,16,128]{2,1,0:T(8,128)(2,1)}, /*index=5*/bf16...) while((s32[]{:T(128)}, f32[3,16,128]{2,1,0:T(8,128)}, ...), condition=%wide.region_71.72_spmd, body=%wide.region_50.71_spmd.sunk | while | flops 360825856 | bytes 144035920 | solution.py:124
  431.5 63.3 %conditional.8 = (f32[3,8,128]{2,1,0:T(8,128)S(1)}) conditional(s32[]{:T(128)} %convert_element_type.696, () %tuple.181, (f32[4,8,128]{2,1,0:T(8,128)S(1)}, f32[1,8,128]{2,1,0:T(8,128)S(1)}, bf16[56,16,128]{2,1,0:T(8,128)(2,1)}, s32[]{:T(128)}, bf16[128,64]{1,0:T(8,128)(2,1)S(1)}, /*index=5*/bf16[64,128]{1,0:T(8,128)(2,1)}, ...), branch_computations={%region_52.52_spmd, %region_53.70_spmd} | conditional | flops 360823808 | bytes 143969536 | solution.py:109
  443.5 4.5 fusion.184
  450.5 5.2 copy.54
  465.8 4.2 fusion.192
  469.9 4.9 copy.56
  474.8 3.6 bitcast_reduce_fusion.2
  484.9 3.8 copy.57
  498.1 63.3 %conditional.8 = (f32[3,8,128]{2,1,0:T(8,128)S(1)}) conditional(s32[]{:T(128)} %convert_element_type.696, () %tuple.181, (f32[4,8,128]{2,1,0:T(8,128)S(1)}, f32[1,8,128]{2,1,0:T(8,128)S(1)}, bf16[56,16,128]{2,1,0:T(8,128)(2,1)}, s32[]{:T(128)}, bf16[128,64]{1,0:T(8,128)(2,1)S(1)}, /*index=5*/bf16[64,128]{1,0:T(8,128)(2,1)}, ...), branch_computations={%region_52.52_spmd, %region_53.70_spmd} | conditional | flops 360823808 | bytes 143969536 | solution.py:109
  510.0 4.5 fusion.184
  517.0 5.2 copy.54
  532.3 4.2 fusion.192
  536.5 4.9 copy.56
  541.4 3.6 bitcast_reduce_fusion.2
  551.5 3.8 copy.57
  563.4 11.7 %scatter_custom_fusion.2 = f32[3,1152]{0,1:T(8,128)S(1)} fusion(s32[2048]{0:T(1024)} %maximum_bitcast_fusion, f32[2048,3]{1,0:T(8,128)S(1)} %bitcast.550, f32[]{:T(128)} %constant.256.clone.1), kind=kCustom, calls=%fused_computation.508 | custom fusion | flops 6144 | bytes 14336 | tf_op jit(solution)/shard_map/vmap()/scatter-add | solution.py:156
  575.6 4.1 collective-permute-start.21
  583.1 3.0 collective-permute-done.22
  (1078 shorter events, 291.3 us)
Async XLA Ops:
  3.3 9.7 %collective-permute-start.1 = (f32[1,1,4,128]{3,2,1,0:T(4,128)S(1)}, f32[1,1,4,128]{3,2,1,0:T(4,128)S(1)}, u32[]{:S(2)}, u32[]{:S(2)}) collective-permute-start(f32[1,1,4,128]{3,2,1,0:T(4,128)S(1)} %fusion.292), channel_id=1, source_target_pairs={{8,0},{16,8},{24,16},{32,24},{40,32},{48,40},{56,48},{64,56},{72,6... | collective-permute-start | bytes 6152 | tf_op jit(solution)/shard_map/ppermute | solution.py:31
  9.1 5.7 collective-permute-start
  11.1 28.5 %copy-start.100 = (s32[2048]{0:T(1024)}, s32[2048]{0:T(1024)S(1)}, u32[]{:S(2)}) copy-start(s32[2048]{0:T(1024)S(1)} %broadcast_clamp_fusion) | copy-start | bytes 24580
  13.0 26.9 %copy-start.112 = (f32[1,16,128]{2,1,0:T(8,128)}, f32[1,16,128]{2,1,0:T(8,128)S(1)}, u32[]{:S(2)}) copy-start(f32[1,16,128]{2,1,0:T(8,128)S(1)} %get-tuple-element.654) | copy-start | bytes 24580
  14.8 6.2 %collective-permute-start.3 = (f32[3,1,4,128]{3,2,1,0:T(4,128)S(1)}, f32[3,1,4,128]{3,2,1,0:T(4,128)S(1)}, u32[]{:S(2)}, u32[]{:S(2)}) collective-permute-start(f32[3,1,4,128]{3,2,1,0:T(4,128)S(1)} %pad_maximum_fusion.18), channel_id=1, source_target_pairs={{1,0},{2,1},{3,2},{4,3},{5,4},{6,5},{7,6},{0,7},{9,8},{10,9},{11,1... | collective-permute-start | bytes 18440 | tf_op jit(solution)/shard_map/ppermute | solution.py:31
  15.5 5.4 collective-permute-start.2
  18.3 22.2 %copy-start.73 = (bf16[28,16,128]{2,1,0:T(8,128)(2,1)}, bf16[28,16,128]{2,1,0:T(8,128)(2,1)S(1)}, u32[]{:S(2)}) copy-start(bf16[28,16,128]{2,1,0:T(8,128)(2,1)S(1)} %slice.447) | copy-start | bytes 344068
  175.4 21.5 %copy-start.152 = (s32[1,1,128]{2,1,0:T(1,128)S(1)}, s32[1,1,128]{2,1,0:T(1,128)}, u32[]{:S(2)}) copy-start(s32[1,1,128]{2,1,0:T(1,128)} %param.27) | copy-start | bytes 1540
  175.5 26.3 %copy-start.130 = (f32[1,1,3,128]{3,1,2,0:T(1,128)S(1)}, f32[1,1,3,128]{3,1,2,0:T(1,128)}, u32[]{:S(2)}) copy-start(f32[1,1,3,128]{3,1,2,0:T(1,128)} %param.25) | copy-start | bytes 4612
  175.5 26.3 %copy-start.136 = (f32[1,1,3,128]{3,1,2,0:T(1,128)S(1)}, f32[1,1,3,128]{3,1,2,0:T(1,128)}, u32[]{:S(2)}) copy-start(f32[1,1,3,128]{3,1,2,0:T(1,128)} %param.26) | copy-start | bytes 4612
  176.2 25.6 %copy-start.147 = (f32[1,128]{1,0:T(1,128)S(1)}, f32[1,128]{1,0:T(1,128)}, u32[]{:S(2)}) copy-start(f32[1,128]{1,0:T(1,128)} %copy-done.146) | copy-start | bytes 1540
  176.2 29.7 %copy-start.123 = (s32[16,8]{1,0:T(8,128)S(1)}, s32[16,8]{1,0:T(8,128)}, u32[]{:S(2)}) copy-start(s32[16,8]{1,0:T(8,128)} %copy-done.122) | copy-start | bytes 1540
  176.2 35.9 %copy-start.104 = (f32[3,16,8]{2,1,0:T(8,128)S(1)}, f32[3,16,8]{2,1,0:T(8,128)}, u32[]{:S(2)}) copy-start(f32[3,16,8]{2,1,0:T(8,128)} %copy-done.103) | copy-start | bytes 4612
  176.6 39.6 %copy-start.118 = (f32[9,3]{1,0:T(8,128)S(1)}, f32[9,3]{1,0:T(8,128)}, u32[]{:S(2)}) copy-start(f32[9,3]{1,0:T(8,128)} %constant.267.clone) | copy-start | bytes 328
  188.4 27.8 %copy-start.101 = (s32[2048]{0:T(1024)S(1)}, s32[2048]{0:T(1024)}, u32[]{:S(2)}) copy-start(s32[2048]{0:T(1024)} %copy-done.100) | copy-start | bytes 24580
  188.7 5.9 %collective-permute-start.4 = (f32[1,1,3456]{2,1,0:T(1,128)S(1)}, f32[1,1,3456]{2,1,0:T(1,128)S(1)}, u32[]{:S(2)}, u32[]{:S(2)}) collective-permute-start(f32[1,1,3456]{2,1,0:T(1,128)S(1)} %reshape.1187), channel_id=1, source_target_pairs={{0,8},{8,16},{16,24},{24,32},{32,40},{40,48},{48,56},{56,64},{64,7... | collective-permute-start | bytes 41480 | tf_op jit(solution)/shard_map/ppermute | solution.py:30
  188.8 5.9 collective-permute-start.5
  194.7 3.9 collective-permute-start.7
  196.9 4.6 collective-permute-start.6
  196.9 19.0 %copy-start.149 = (f32[128]{0:T(128)}, f32[128]{0:T(128)S(1)}, u32[]{:S(2)}) copy-start(f32[128]{0:T(128)S(1)} %fusion.306) | copy-start | bytes 1540
  197.1 25.0 %copy-start.113 = (f32[1,16,128]{2,1,0:T(8,128)S(1)}, f32[1,16,128]{2,1,0:T(8,128)}, u32[]{:S(2)}) copy-start(f32[1,16,128]{2,1,0:T(8,128)} %copy-done.112) | copy-start | bytes 24580
  197.2 18.7 %copy-start.97 = (f32[3,16,8]{2,1,0:T(8,128)}, f32[3,16,8]{2,1,0:T(8,128)S(1)}, u32[]{:S(2)}) copy-start(f32[3,16,8]{2,1,0:T(8,128)S(1)} %reduce_sum.627) | copy-start | bytes 4612
  201.8 32.7 %copy-start.133 = (f32[1,1,1,3,128]{4,3,2,1,0:T(4,128)}, f32[1,1,1,3,128]{4,3,2,1,0:T(4,128)S(1)}, u32[]{:S(2)}) copy-start(f32[1,1,1,3,128]{4,3,2,1,0:T(4,128)S(1)} %get-tuple-element.554) | copy-start | bytes 4612
  201.9 5.3 collective-permute-start.9
  205.9 5.7 collective-permute-start.8
  205.9 28.6 %copy-start.120 = (f32[16,8]{1,0:T(8,128)}, f32[16,8]{1,0:T(8,128)S(1)}, u32[]{:S(2)}) copy-start(f32[16,8]{1,0:T(8,128)S(1)} %divide_multiply_fusion) | copy-start | bytes 1540
  211.6 1.4 collective-permute-start.11
  211.6 4.3 collective-permute-start.10
  222.7 12.1 %copy-start.74 = (bf16[28,16,128]{2,1,0:T(8,128)(2,1)S(1)}, bf16[28,16,128]{2,1,0:T(8,128)(2,1)}, u32[]{:S(2)}) copy-start(bf16[28,16,128]{2,1,0:T(8,128)(2,1)} %copy-done.73) | copy-start | bytes 344068
  370.1 24.1 %copy-start.131 = (f32[1,1,3,128]{3,1,2,0:T(1,128)S(1)}, f32[1,1,3,128]{3,1,2,0:T(1,128)}, u32[]{:S(2)}) copy-start(f32[1,1,3,128]{3,1,2,0:T(1,128)} %param.25) | copy-start | bytes 4612
  370.1 24.1 %copy-start.134 = (f32[1,1,1,3,128]{4,3,2,1,0:T(4,128)S(1)}, f32[1,1,1,3,128]{4,3,2,1,0:T(4,128)}, u32[]{:S(2)}) copy-start(f32[1,1,1,3,128]{4,3,2,1,0:T(4,128)} %copy-done.133) | copy-start | bytes 4612
  370.1 24.1 %copy-start.137 = (f32[1,1,3,128]{3,1,2,0:T(1,128)S(1)}, f32[1,1,3,128]{3,1,2,0:T(1,128)}, u32[]{:S(2)}) copy-start(f32[1,1,3,128]{3,1,2,0:T(1,128)} %param.26) | copy-start | bytes 4612
  370.1 24.1 %copy-start.142 = (f32[3,128]{1,0:T(4,128)S(1)}, f32[3,128]{1,0:T(4,128)}, u32[]{:S(2)}) copy-start(f32[3,128]{1,0:T(4,128)} %copy-done.141) | copy-start | bytes 4612
  370.2 24.1 %copy-start.150 = (f32[128]{0:T(128)S(1)}, f32[128]{0:T(128)}, u32[]{:S(2)}) copy-start(f32[128]{0:T(128)} %copy-done.149) | copy-start | bytes 1540
  370.9 23.4 %copy-start.148 = (f32[1,128]{1,0:T(1,128)S(1)}, f32[1,128]{1,0:T(1,128)}, u32[]{:S(2)}) copy-start(f32[1,128]{1,0:T(1,128)} %copy-done.146) | copy-start | bytes 1540
  370.9 33.8 %copy-start.98 = (f32[3,16,8]{2,1,0:T(8,128)S(1)}, f32[3,16,8]{2,1,0:T(8,128)}, u32[]{:S(2)}) copy-start(f32[3,16,8]{2,1,0:T(8,128)} %copy-done.97) | copy-start | bytes 4612
  370.9 33.8 %copy-start.105 = (f32[3,16,8]{2,1,0:T(8,128)S(1)}, f32[3,16,8]{2,1,0:T(8,128)}, u32[]{:S(2)}) copy-start(f32[3,16,8]{2,1,0:T(8,128)} %copy-done.103) | copy-start | bytes 4612
  370.9 33.8 %copy-start.109 = (f32[3,16,8]{2,1,0:T(8,128)S(1)}, f32[3,16,8]{2,1,0:T(8,128)}, u32[]{:S(2)}) copy-start(f32[3,16,8]{2,1,0:T(8,128)} %copy-done.108) | copy-start | bytes 4612
  370.9 33.8 %copy-start.111 = (f32[3,16,8]{2,1,0:T(8,128)S(1)}, f32[3,16,8]{2,1,0:T(8,128)}, u32[]{:S(2)}) copy-start(f32[3,16,8]{2,1,0:T(8,128)} %copy-done.110) | copy-start | bytes 4612
  370.9 33.8 %copy-start.121 = (f32[16,8]{1,0:T(8,128)S(1)}, f32[16,8]{1,0:T(8,128)}, u32[]{:S(2)}) copy-start(f32[16,8]{1,0:T(8,128)} %copy-done.120) | copy-start | bytes 1540
  371.3 37.5 %copy-start.119 = (f32[9,3]{1,0:T(8,128)S(1)}, f32[9,3]{1,0:T(8,128)}, u32[]{:S(2)}) copy-start(f32[9,3]{1,0:T(8,128)} %constant.267.clone) | copy-start | bytes 328
  383.1 25.7 %copy-start.102 = (s32[2048]{0:T(1024)S(1)}, s32[2048]{0:T(1024)}, u32[]{:S(2)}) copy-start(s32[2048]{0:T(1024)} %copy-done.100) | copy-start | bytes 24580
  383.4 5.9 %collective-permute-start.12 = (f32[1,1,3456]{2,1,0:T(1,128)S(1)}, f32[1,1,3456]{2,1,0:T(1,128)S(1)}, u32[]{:S(2)}, u32[]{:S(2)}) collective-permute-start(f32[1,1,3456]{2,1,0:T(1,128)S(1)} %reshape.1198), channel_id=1, source_target_pairs={{0,8},{8,16},{16,24},{24,32},{32,40},{40,48},{48,56},{56,64},{64,7... | collective-permute-start | bytes 41480 | tf_op jit(solution)/shard_map/ppermute | solution.py:30
  383.5 5.8 collective-permute-start.13
  389.3 1.7 collective-permute-start.15
  389.4 4.7 collective-permute-start.14
  390.0 24.7 %copy-start.114 = (f32[1,16,128]{2,1,0:T(8,128)S(1)}, f32[1,16,128]{2,1,0:T(8,128)}, u32[]{:S(2)}) copy-start(f32[1,16,128]{2,1,0:T(8,128)} %copy-done.112) | copy-start | bytes 24580
  390.1 18.4 %copy-start.106 = (f32[3,16,8]{2,1,0:T(8,128)}, f32[3,16,8]{2,1,0:T(8,128)S(1)}, u32[]{:S(2)}) copy-start(f32[3,16,8]{2,1,0:T(8,128)S(1)} %reduce_sum.632) | copy-start | bytes 4612
  394.3 32.8 %copy-start.139 = (f32[1,1,1,3,128]{4,3,2,1,0:T(4,128)}, f32[1,1,1,3,128]{4,3,2,1,0:T(4,128)S(1)}, u32[]{:S(2)}) copy-start(f32[1,1,1,3,128]{4,3,2,1,0:T(4,128)S(1)} %get-tuple-element.552) | copy-start | bytes 4612
  394.3 5.5 collective-permute-start.17
  398.5 5.7 collective-permute-start.16
  404.2 1.4 collective-permute-start.19
  404.2 4.3 collective-permute-start.18
  562.2 19.7 %copy-start.99 = (f32[3,16,8]{2,1,0:T(8,128)S(1)}, f32[3,16,8]{2,1,0:T(8,128)}, u32[]{:S(2)}) copy-start(f32[3,16,8]{2,1,0:T(8,128)} %copy-done.97) | copy-start | bytes 4612
  562.2 19.8 %copy-start.107 = (f32[3,16,8]{2,1,0:T(8,128)S(1)}, f32[3,16,8]{2,1,0:T(8,128)}, u32[]{:S(2)}) copy-start(f32[3,16,8]{2,1,0:T(8,128)} %copy-done.106) | copy-start | bytes 4612
  563.0 23.3 %copy-start.132 = (f32[1,1,3,128]{3,1,2,0:T(1,128)S(1)}, f32[1,1,3,128]{3,1,2,0:T(1,128)}, u32[]{:S(2)}) copy-start(f32[1,1,3,128]{3,1,2,0:T(1,128)} %param.25) | copy-start | bytes 4612
  563.0 23.3 %copy-start.135 = (f32[1,1,1,3,128]{4,3,2,1,0:T(4,128)S(1)}, f32[1,1,1,3,128]{4,3,2,1,0:T(4,128)}, u32[]{:S(2)}) copy-start(f32[1,1,1,3,128]{4,3,2,1,0:T(4,128)} %copy-done.133) | copy-start | bytes 4612
  563.0 23.3 %copy-start.138 = (f32[1,1,3,128]{3,1,2,0:T(1,128)S(1)}, f32[1,1,3,128]{3,1,2,0:T(1,128)}, u32[]{:S(2)}) copy-start(f32[1,1,3,128]{3,1,2,0:T(1,128)} %param.26) | copy-start | bytes 4612
  563.0 23.3 %copy-start.140 = (f32[1,1,1,3,128]{4,3,2,1,0:T(4,128)S(1)}, f32[1,1,1,3,128]{4,3,2,1,0:T(4,128)}, u32[]{:S(2)}) copy-start(f32[1,1,1,3,128]{4,3,2,1,0:T(4,128)} %copy-done.139) | copy-start | bytes 4612
  563.0 23.3 %copy-start.151 = (f32[128]{0:T(128)S(1)}, f32[128]{0:T(128)}, u32[]{:S(2)}) copy-start(f32[128]{0:T(128)} %copy-done.149) | copy-start | bytes 1540
  575.5 5.9 %collective-permute-start.20 = (f32[1,1,3456]{2,1,0:T(1,128)S(1)}, f32[1,1,3456]{2,1,0:T(1,128)S(1)}, u32[]{:S(2)}, u32[]{:S(2)}) collective-permute-start(f32[1,1,3456]{2,1,0:T(1,128)S(1)} %reshape.1209), channel_id=1, source_target_pairs={{0,8},{8,16},{16,24},{24,32},{32,40},{40,48},{48,56},{56,64},{64,7... | collective-permute-start | bytes 41480 | tf_op jit(solution)/shard_map/ppermute | solution.py:30
  575.6 5.8 collective-permute-start.21
  581.4 1.7 collective-permute-start.23
  581.4 4.7 collective-permute-start.22
  (236 other events, 611.4 us)
where the time goes:
time: 597 us; the launch traced here: 588 us
  local copies, waits for them, and re-layouts  277 us (46%)
  other arithmetic  175 us (29%)
  matrix products  56.3 us (9%)
  waiting for transfers between devices  36.6 us (6%)
  starting transfers between devices  31.7 us (5%)
  loops' own time  9.07 us (2%)
    dot_general x64, matrix products, matmul(): jnp.dot(left.astype(jnp.float32), right.astype(jnp.float32), preferred_el...  56.3 us
    cond x468, local copies, waits for them, and re-layouts  43.9 us
    gather x3, local copies, waits for them, and re-layouts, build_edges(): far_kind = ghost_kinds[index]  35.3 us
    scatter-add x3, other arithmetic, split_terms(): jax.ops.segment_sum(comp, index, num_segments=9 * atoms)  35.2 us
    mul x12, local copies, waits for them, and re-layouts, edge_energy(): prod = spread_orders(value) * sph[:, None, :] * env_rep  34.9 us
    reshape x6, local copies, waits for them, and re-layouts, edge_energy(): env_rep = jnp.repeat(env, SLOTS, axis=2)  31.3 us
    ppermute x12, waiting for transfers between devices, padded(): before = lax.ppermute(last, axis, up)  30.4 us
    mul x12, other arithmetic, edge_energy(): prod = spread_orders(value) * sph[:, None, :] * env_rep  29.5 us
  transfers between devices with their start and end apart: 24, of which 18 were waited for; matrix products, arithmetic and copies ran while one was open for 2% of the time, Pallas kernels for 0%

commit v1 on v0

v1 whole, which is shorter than its diff:
```python
import math

import jax
import jax.numpy as jnp
from jax import lax
from jax.experimental import pallas as pl
from jax.experimental.pallas import tpu as pltpu
from jax.sharding import PartitionSpec as P

MESH = pl.DeviceIdType.MESH
F32 = jnp.float32
BF16 = jnp.bfloat16

C = 64
HID = 128
EMB = 28
NBASIS = 8
NS = 4
SLOTS = 16
STEPS = 2
CENTERS = 8
NB = 16
LANES = 128
EVALS = STEPS + 1
GB = 4

TIME_STEP = 0.2
CUTOFF = 4.5
SOFTEN = 0.04
MASSES = (3.0, 2.0, 1.5, 1.0)

R3 = math.sqrt(3.0)
R5 = math.sqrt(5.0)
R15 = math.sqrt(15.0)


def dot(a, b):
    return jnp.dot(a, b, preferred_element_type=F32)


def iota(shape, dim):
    return lax.broadcasted_iota(jnp.int32, shape, dim)


def column(row, size):
    square = jnp.broadcast_to(row, (size, size))
    diag = jnp.where(iota((size, size), 0) == iota((size, size), 1), square, 0.0)
    return jnp.broadcast_to(jnp.sum(diag, axis=1, keepdims=True), (size, LANES))


def lane_pick(row, index):
    return jnp.take_along_axis(
        jnp.broadcast_to(row, index.shape), index, axis=1, mode="promise_in_bounds"
    )


def gate(x):
    sig = 0.5 * jnp.tanh(0.5 * x) + 0.5
    act = x * sig
    return act, sig * (1.0 + (x - act))


def kernel(
    nx, ny,
    pos_ref, vel_ref, kind_ref, nbr_ref, emb_ref, w_in_ref, w_two_ref, w_val_ref, w_env_ref,
    w_mix_ref, w_lat_ref, w_out_ref,
    pos_out, vel_out, frc_out,
    pbuf, psend, fbuf, fsend, onehot, slotmask, zrest, zfirst, geo, back, gdense,
    w_ve, w_ve_t, w_mix_t, w_two_t, w_in_t, w_hid_rows, w_hid_col, w_out_col, same, same16, seg,
    state, send_sem, recv_sem,
):
    mx, my = lax.axis_index("dx"), lax.axis_index("dy")
    others = [o for o in range(9) if o != 4]

    def device(o):
        p, q = o // 3 - 1, o % 3 - 1
        return (lax.rem(mx + (p + nx), nx), lax.rem(my + (q + ny), ny))

    barrier = pltpu.get_barrier_semaphore()
    for o in others:
        pl.semaphore_signal(barrier, inc=1, device_id=device(o), device_id_type=MESH)

    def pos_copy(t, o):
        return pltpu.make_async_remote_copy(
            src_ref=psend.at[t], dst_ref=pbuf.at[t, 8 - o],
            send_sem=send_sem.at[t, 0, o], recv_sem=recv_sem.at[t, 0, 8 - o],
            device_id=device(o), device_id_type=MESH,
        )

    def frc_copy(t, o):
        return pltpu.make_async_remote_copy(
            src_ref=fsend.at[t, o], dst_ref=fbuf.at[t, 8 - o],
            send_sem=send_sem.at[t, 1, o], recv_sem=recv_sem.at[t, 1, 8 - o],
            device_id=device(o), device_id_type=MESH,
        )

    kinds = kind_ref[0].astype(F32)
    start = jnp.concatenate([pos_ref[0, 0], kinds, jnp.zeros((4, LANES), F32)], axis=0)
    psend[0] = start
    state[0] = start
    state[1] = jnp.concatenate([vel_ref[0, 0], jnp.zeros((5, LANES), F32)], axis=0)
    pl.semaphore_wait(barrier, 8)
    for o in others:
        pos_copy(0, o).start()

    mass = jnp.zeros((1, LANES), F32)
    for kind in range(NS):
        mass = mass + jnp.where(kinds == float(kind), MASSES[kind], 0.0)
    inv_mass = 1.0 / mass

    w_ve[0 : 3 * C, :] = w_val_ref[...]
    w_ve[3 * C : 6 * C, :] = w_env_ref[...]
    w_ve_t[...] = jnp.concatenate(
        [w_val_ref[...].astype(F32), w_env_ref[...].astype(F32)], axis=0
    ).T.astype(BF16)
    w_mix_t[...] = w_mix_ref[...].astype(F32).T.astype(BF16)
    w_two_t[...] = w_two_ref[...].astype(F32).T.astype(BF16)
    w_in_t[...] = w_in_ref[...].astype(F32).T[0:16].astype(BF16)
    out_col = column(w_out_ref[...].reshape(1, C), C)
    w_out_col[...] = out_col
    w_hid = jnp.sum(w_lat_ref[...].astype(F32) * out_col, axis=0, keepdims=True)
    w_hid_col[...] = column(w_hid, HID)
    hid_hi = w_hid.astype(BF16).astype(F32)
    row16 = iota((16, LANES), 0)
    w_hid_rows[...] = jnp.where(
        row16 == 0, hid_hi, jnp.where(row16 == 1, w_hid - hid_hi, 0.0)
    ).astype(BF16)
    lane_r, lane_c = iota((LANES, LANES), 0), iota((LANES, LANES), 1)
    together = jnp.where(lane_r // SLOTS == lane_c // SLOTS, 1.0 / SLOTS, 0.0)
    same[...] = together
    same16[...] = together.astype(BF16)
    seg[...] = jnp.where(lane_r // SLOTS == lane_c % CENTERS, 1.0, 0.0).astype(BF16)

    nbrs = nbr_ref[0, 0]
    valid = jnp.where(nbrs >= 0, 1.0, 0.0)
    index = jnp.maximum(nbrs, 0)
    atom = jnp.bitwise_and(index, LANES - 1)
    slot = jnp.right_shift(index, 7)
    gdense[0] = atom.astype(F32)
    gdense[1] = slot.astype(F32)
    row_b, lane_b = iota((NB, LANES), 0), iota((NB, LANES), 1)
    centre_index = row_b * CENTERS + lane_b // SLOTS
    owner = jnp.where(lane_b // CENTERS == row_b, 1.0, 0.0)
    slot_x = (slot // 3).astype(F32) - 1.0
    slot_y = jnp.remainder(slot, 3).astype(F32) - 1.0

    def one_hots(b, carry):
        onehot[b] = jnp.where(
            lane_r.astype(F32) == gdense[0, pl.ds(b, 1), :], 1.0, 0.0
        ).astype(BF16)
        slotmask[b] = jnp.where(row16.astype(F32) == gdense[1, pl.ds(b, 1), :], 1.0, 0.0)
        return carry

    lax.fori_loop(0, NB, one_hots, 0)

    for o in others:
        pos_copy(0, o).wait_recv()
    pbuf[0, 4] = start
    far_kind = jnp.zeros((NB, LANES), F32)
    for o in range(9):
        far_kind = jnp.where(slot == o, lane_pick(pbuf[0, o, 3:4, :], atom), far_kind)
    gdense[0] = lane_pick(kinds, centre_index)
    gdense[1] = far_kind
    emb_t = emb_ref[...].astype(F32).T.astype(BF16)
    row4 = iota((NS, LANES), 0).astype(F32)

    def embeddings(b, carry):
        looked = [
            dot(emb_t, jnp.where(row4 == gdense[i, pl.ds(b, 1), :], 1.0, 0.0).astype(BF16))
            for i in range(2)
        ]
        both = jnp.concatenate(looked, axis=0)
        zfirst[b] = both[0:8]
        zrest[b] = both[8 : 2 * EMB].astype(BF16)
        return carry

    lax.fori_loop(0, NB, embeddings, 0)

    row8 = iota((8, LANES), 0)

    def group(g, carry):
        blocks = [g * GB + j for j in range(GB)]

        def wide(parts):
            return jnp.concatenate(parts, axis=1)

        def part(x, j):
            return x[:, j * LANES : (j + 1) * LANES]

        cut = wide([geo[b, 16:17, :] for b in blocks])
        top = wide([jnp.concatenate([geo[b, 0:8, :], zfirst[b]], axis=0) for b in blocks])
        zin = jnp.concatenate([top.astype(BF16), wide([zrest[b] for b in blocks])], axis=0)
        hidden, slope1 = gate(dot(w_in_ref[...], zin))
        pre = dot(w_two_ref[...], hidden.astype(BF16))
        latent16 = (pre * cut).astype(BF16)
        value_envw = dot(w_ve[...], latent16)
        value = value_envw[0 : 3 * C]
        envw = value_envw[3 * C : 6 * C].astype(BF16)

        gram = []
        sphs = []
        for b in blocks:
            sph = geo[b, 8:16, :]
            tall = sph.T.astype(BF16)
            g1 = dot(tall, jnp.where(row8 < 3, sph, 0.0).astype(BF16))
            g2 = dot(tall, jnp.where(row8 < 3, 0.0, sph).astype(BF16))
            sphs.append(sph.astype(BF16))
            gram.append(
                [same16[...], (g1 * same[...]).astype(BF16), (g2 * same[...]).astype(BF16)]
            )

        def mix_slots(x):
            return wide(
                [
                    jnp.concatenate(
                        [dot(part(x, j)[l * C : (l + 1) * C], gram[j][l]) for l in range(3)], axis=0
                    )
                    for j in range(GB)
                ]
            )

        env_at = mix_slots(envw)
        mixed = jnp.concatenate([latent16, (value * env_at).astype(BF16)], axis=0)
        hidden2, slope2 = gate(dot(w_mix_ref[...], mixed))
        readout = dot(w_hid_rows[...], hidden2.astype(BF16))
        readout = readout[0:1] + readout[1:2]

        d_a2 = slope2 * (wide([w_hid_col[...]] * GB) * cut)
        d_mixed = dot(w_mix_t[...], d_a2.astype(BF16))
        d_scal = d_mixed[C : 4 * C]
        d_value = (d_scal * env_at).astype(BF16)
        d_envat = (d_scal * value).astype(BF16)
        d_envw = mix_slots(d_envat).astype(BF16)
        energy_part = wide([w_out_col[...]] * GB) * cut
        d_latent = d_mixed[0:C] + dot(
            w_ve_t[...], jnp.concatenate([d_value, d_envw], axis=0)
        ) + energy_part
        d_cut = readout + jnp.sum(pre * (d_latent + energy_part), axis=0, keepdims=True)
        d_hidden = dot(w_two_t[...], (d_latent * cut).astype(BF16))
        d_basis = dot(w_in_t[...], (d_hidden * slope1).astype(BF16))

        for j, b in enumerate(blocks):
            d_sph = []
            for l in (1, 2):
                dq, ew = part(d_envat, j)[l * C : (l + 1) * C], part(envw, j)[l * C : (l + 1) * C]
                left, right = jnp.concatenate([dq, ew], axis=0), jnp.concatenate([ew, dq], axis=0)
                pair = lax.dot_general(
                    left, right, (((0,), (0,)), ((), ())), preferred_element_type=F32
                )
                d_sph.append(dot(sphs[j], (pair * same[...]).astype(BF16)))
            back[b, 0:8, :] = part(d_basis, j)[0:8]
            back[b, 8:16, :] = jnp.where(row8 < 3, d_sph[0], d_sph[1])
            back[b, 16:17, :] = part(d_cut, j)
        return carry

    def evaluate(t, carry):
        @pl.when(t > 0)
        def _():
            psend[t] = state[0]
            for o in others:
                pos_copy(t, o).start()
            for o in others:
                pos_copy(t, o).wait_recv()
            pbuf[t, 4] = state[0]

        here = state[0]
        rel = []
        for k in range(3):
            far = jnp.zeros((NB, LANES), F32)
            for o in range(9):
                far = jnp.where(slot == o, lane_pick(pbuf[t, o, k : k + 1, :], atom), far)
            if k == 0:
                far = far + slot_x
            if k == 1:
                far = far + slot_y
            rel.append(far - lane_pick(here[k : k + 1], centre_index))
        dist_sq = rel[0] * rel[0] + rel[1] * rel[1] + rel[2] * rel[2] + SOFTEN
        dist = jnp.sqrt(dist_sq)
        inv = 1.0 / dist
        ux, uy, uz = rel[0] * inv, rel[1] * inv, rel[2] * inv
        fall = 1.0 - dist_sq * (1.0 / (CUTOFF * CUTOFF))
        cut = valid * fall * fall
        theta = dist * (math.pi / CUTOFF)
        sin1, cos1 = jnp.sin(theta), jnp.cos(theta)
        sines, cosines = [sin1], [cos1]
        for n in range(1, NBASIS):
            s, c = sines[-1], cosines[-1]
            sines.append(s * cos1 + c * sin1)
            cosines.append(c * cos1 - s * sin1)
        for n in range(NBASIS):
            geo[:, n, :] = sines[n] * inv * cut
        sph = (
            R3 * ux, R3 * uy, R3 * uz, R15 * ux * uy, R15 * uy * uz,
            0.5 * R5 * (3.0 * uz * uz - 1.0), R15 * ux * uz, 0.5 * R15 * (ux * ux - uy * uy),
        )
        for m in range(8):
            geo[:, 8 + m, :] = sph[m]
        geo[:, 16, :] = cut

        lax.fori_loop(0, NB // GB, group, 0)

        d1, d2, d3, d4, d5, d6, d7, d8 = [back[:, 8 + m, :] for m in range(8)]
        du = (
            R3 * d1 + R15 * (uy * d4 + uz * d7 + ux * d8),
            R3 * d2 + R15 * (ux * d4 + uz * d5 - uy * d8),
            R3 * d3 + R15 * (uy * d5 + ux * d7) + (3.0 * R5) * (uz * d6),
        )
        by_sin = jnp.zeros((NB, LANES), F32)
        by_cos = jnp.zeros((NB, LANES), F32)
        for n in range(NBASIS):
            d_basis = back[:, n, :]
            by_sin = by_sin + d_basis * sines[n]
            by_cos = by_cos + (d_basis * cosines[n]) * ((n + 1) * math.pi / CUTOFF)
        by_sin = by_sin * inv
        d_cut = back[:, 16, :] + by_sin
        d_dist = cut * inv * (by_cos - by_sin) - inv * (du[0] * ux + du[1] * uy + du[2] * uz)
        d_sq = 0.5 * inv * d_dist - d_cut * (valid * fall) * (2.0 / (CUTOFF * CUTOFF))
        grads = [(du[k] * inv + 2.0 * rel[k] * d_sq) * valid for k in range(3)]

        split = []
        for k in range(3):
            high = grads[k].astype(BF16).astype(F32)
            gdense[k] = high
            gdense[3 + k] = grads[k] - high
        segs = dot(gdense[...].reshape(6 * NB, LANES).astype(BF16), seg[...])
        centre = [
            jnp.sum(
                (segs[k * NB : (k + 1) * NB] + segs[(3 + k) * NB : (4 + k) * NB]) * owner,
                axis=0, keepdims=True,
            )
            for k in range(3)
        ]
        scattered = jnp.zeros((6 * 16, LANES), F32)
        for b in range(NB):
            left = jnp.concatenate(
                [gdense[i, b : b + 1, :] * slotmask[b] for i in range(6)], axis=0
            ).astype(BF16)
            scattered = scattered + lax.dot_general(
                left, onehot[b], (((1,), (1,)), ((), ())), preferred_element_type=F32
            )
        ghost = [
            scattered[k * 16 : (k + 1) * 16] + scattered[(3 + k) * 16 : (4 + k) * 16]
            for k in range(3)
        ]
        for k in range(3):
            fsend[t, :, k, :] = ghost[k][0:9]
        for o in others:
            frc_copy(t, o).start()
        own = jnp.concatenate(
            [centre[k] - ghost[k][4:5] for k in range(3)] + [jnp.zeros((5, LANES), F32)], axis=0
        )
        for o in others:
            frc_copy(t, o).wait_recv()
        back_sum = fbuf[t, 0]
        for o in others[1:]:
            back_sum = back_sum + fbuf[t, o]
        force = jnp.where(row8 < 3, own - back_sum, 0.0)

        half = (0.5 * TIME_STEP) * inv_mass
        speed = state[1]
        speed = speed + jnp.where(t > 0, 1.0, 0.0) * (half * force)
        more = jnp.where(t < STEPS, 1.0, 0.0)
        speed = speed + more * (half * force)
        state[1] = speed
        state[0] = here + (more * TIME_STEP) * speed
        state[2] = force
        for o in others:
            pos_copy(t, o).wait_send()
            frc_copy(t, o).wait_send()
        return carry

    lax.fori_loop(0, EVALS, evaluate, 0)
    pos_out[0, 0] = state[0, 0:3, :]
    vel_out[0, 0] = state[1, 0:3, :]
    frc_out[0, 0] = state[2, 0:3, :]


def solution(mesh):
    nx, ny = mesh.shape["dx"], mesh.shape["dy"]

    def per_device(*args):
        def body(*refs):
            kernel(nx, ny, *refs)

        vmem = pl.BlockSpec(memory_space=pltpu.VMEM)
        out = jax.ShapeDtypeStruct((1, 1, 3, LANES), F32)
        return pl.pallas_call(
            body,
            out_shape=(out, out, out),
            in_specs=[vmem] * len(args),
            out_specs=(vmem, vmem, vmem),
            scratch_shapes=[
                pltpu.VMEM((EVALS, 9, 8, LANES), F32),
                pltpu.VMEM((EVALS, 8, LANES), F32),
                pltpu.VMEM((EVALS, 9, 8, LANES), F32),
                pltpu.VMEM((EVALS, 9, 8, LANES), F32),
                pltpu.VMEM((NB, LANES, LANES), BF16),
                pltpu.VMEM((NB, 16, LANES), F32),
                pltpu.VMEM((NB, 48, LANES), BF16),
                pltpu.VMEM((NB, 8, LANES), F32),
                pltpu.VMEM((NB, 24, LANES), F32),
                pltpu.VMEM((NB, 24, LANES), F32),
                pltpu.VMEM((6, NB, LANES), F32),
                pltpu.VMEM((6 * C, C), BF16),
                pltpu.VMEM((C, 6 * C), BF16),
                pltpu.VMEM((4 * C, HID), BF16),
                pltpu.VMEM((HID, C), BF16),
                pltpu.VMEM((16, HID), BF16),
                pltpu.VMEM((16, HID), BF16),
                pltpu.VMEM((HID, LANES), F32),
                pltpu.VMEM((C, LANES), F32),
                pltpu.VMEM((LANES, LANES), F32),
                pltpu.VMEM((LANES, LANES), BF16),
                pltpu.VMEM((LANES, LANES), BF16),
                pltpu.VMEM((3, 8, LANES), F32),
                pltpu.SemaphoreType.DMA((EVALS, 2, 9)),
                pltpu.SemaphoreType.DMA((EVALS, 2, 9)),
            ],
            compiler_params=pltpu.CompilerParams(
                collective_id=0, has_side_effects=True, vmem_limit_bytes=48 * 1024 * 1024
            ),
        )(*args)

    grid4 = P("dx", "dy", None, None)
    in_specs = (grid4, grid4, P("dx", "dy", None), grid4) + (P(),) * 8
    return jax.shard_map(
        per_device, mesh=mesh, in_specs=in_specs, out_specs=(grid4, grid4, grid4), check_vma=False
    )
```

time: 597 us -> 74.3 us (0.12)
  the two profiles are of different devices: /device:TPU:16 before, /device:TPU:1 now
where the time goes in v1:
time: 74.3 us; the launch traced here: 74.1 us
  Pallas kernels  68.6 us (92%)
  local copies, waits for them, and re-layouts  4.71 us (6%)
    pallas_call x1, Pallas kernels, per_device(): pl.pallas_call(body, out_shape=(out, out, out), in_specs=[vmem] * len(arg...  68.6 us
    unnamed x23, local copies, waits for them, and re-layouts  3.02 us
    pallas_call x3, local copies, waits for them, and re-layouts, per_device(): pl.pallas_call(body, out_shape=(out, out, out), in_specs=[vmem] * len(arg...  1.69 us

profile of v1, /device:TPU:1, one launch (start us, length us, event | category | flops | bytes accessed | tf_op | source)
XLA Modules:
  0.0 74.1 jit_solution(6459927714748163939)
XLA Ops:
  0.6 0.0 copy-start.7
  0.6 0.7 copy.15.refs_0_
  1.3 0.7 copy.16.refs_1_
  2.0 0.0 copy-start.8
  2.0 0.8 %copy.17.refs_5_ = bf16[128,64]{1,0:T(8,128)(2,1)S(1)} copy(bf16[128,64]{0,1:T(8,128)(2,1)} %param.17) | data formatting | bytes 32768 | tf_op args[5]
  2.8 0.0 copy-done.7
  2.9 0.0 copy-start
  2.9 0.1 copy.18.refs_7_
  3.0 0.0 copy-done.8
  3.0 0.0 copy-start.1
  3.0 0.0 copy-start.2
  3.0 0.0 copy-start.3
  3.0 0.0 copy-start.4
  3.0 0.0 copy-start.5
  3.0 0.0 copy-start.6
  3.1 0.1 copy.19.refs_8_
  3.2 0.5 copy-done
  3.7 0.0 copy-done.1
  3.7 0.0 copy-done.2
  3.7 0.0 copy-done.3
  3.7 0.0 copy-done.4
  3.7 0.0 copy-done.5
  3.7 0.0 copy-done.6
  3.7 68.6 %shard_map.139 = (f32[1,1,3,128]{3,2,1,0:T(4,128)S(1)}, f32[1,1,3,128]{3,2,1,0:T(4,128)S(1)}, f32[1,1,3,128]{3,2,1,0:T(4,128)S(1)}) custom-call(f32[1,1,3,128]{3,2,1,0:T(4,128)S(1)} %copy.15.refs_0_, f32[1,1,3,128]{3,2,1,0:T(4,128)S(1)} %copy.16.refs_1_, s32[1,1,128]{2,1,0:T(1,128)S(1)} %copy-done.5, s32[1,1,16,128]{3,2,1,0:T(8,128)S(1)} %copy-done.3, ...), custom_call_target="tpu_custom_call" | custom-call | tf_op jit(solution)/shard_map/pallas_call | solution.py:387
  72.4 0.6 copy.20
  72.9 0.6 copy.21
  73.5 0.6 copy.22
Async XLA Ops:
  0.6 2.2 %copy-start.7 = (bf16[192,64]{0,1:T(8,128)(2,1)S(1)}, bf16[192,64]{0,1:T(8,128)(2,1)}, u32[]{:S(2)}) copy-start(bf16[192,64]{0,1:T(8,128)(2,1)} %param.19) | copy-start | bytes 73732
  2.0 1.0 %copy-start.8 = (bf16[192,64]{0,1:T(8,128)(2,1)S(1)}, bf16[192,64]{0,1:T(8,128)(2,1)}, u32[]{:S(2)}) copy-start(bf16[192,64]{0,1:T(8,128)(2,1)} %param.20) | copy-start | bytes 73732
  2.9 0.8 %copy-start = (bf16[128,256]{1,0:T(8,128)(2,1)S(1)}, bf16[128,256]{1,0:T(8,128)(2,1)}, u32[]{:S(2)}) copy-start(bf16[128,256]{1,0:T(8,128)(2,1)} %refs_9_.1) | copy-start | bytes 196612
  3.0 0.7 copy-start.1
  3.0 0.7 copy-start.2
  3.0 0.7 copy-start.3
  3.0 0.7 copy-start.4
  3.0 0.7 copy-start.5
  3.0 0.7 copy-start.6

commit v2 on v1

v2 whole, which is shorter than its diff:
```python
import math

import jax
import jax.numpy as jnp
from jax import lax
from jax.experimental import pallas as pl
from jax.experimental.pallas import tpu as pltpu
from jax.sharding import PartitionSpec as P

MESH = pl.DeviceIdType.MESH
F32 = jnp.float32
BF16 = jnp.bfloat16

C = 64
HID = 128
EMB = 28
NBASIS = 8
NS = 4
SLOTS = 16
STEPS = 2
CENTERS = 8
NB = 16
LANES = 128
EVALS = STEPS + 1
GB = 8
LAG = 0

VMEM_BYTES = 63 * 1024 * 1024

TIME_STEP = 0.2
CUTOFF = 4.5
SOFTEN = 0.04
MASSES = (3.0, 2.0, 1.5, 1.0)

R3 = math.sqrt(3.0)
R5 = math.sqrt(5.0)
R15 = math.sqrt(15.0)


def dot(a, b):
    return jnp.dot(a, b, preferred_element_type=F32)


def iota(shape, dim):
    return lax.broadcasted_iota(jnp.int32, shape, dim)


def column(row, size):
    square = jnp.broadcast_to(row, (size, size))
    diag = jnp.where(iota((size, size), 0) == iota((size, size), 1), square, 0.0)
    return jnp.broadcast_to(jnp.sum(diag, axis=1, keepdims=True), (size, LANES))


def lane_pick(row, index):
    return jnp.take_along_axis(
        jnp.broadcast_to(row, index.shape), index, axis=1, mode="promise_in_bounds"
    )


def gate(half):
    t = jnp.tanh(half)
    up = 1.0 + t
    act = half * up
    return act.astype(BF16), (up + act * (1.0 - t)).astype(BF16)


def kernel(
    nx, ny,
    pos_hbm, vel_hbm, kind_hbm, nbr_hbm, emb_hbm, w_in_hbm, w_two_hbm, w_val_hbm, w_env_hbm,
    w_mix_hbm, w_lat_hbm, w_out_hbm,
    pos_out, vel_out, frc_out,
    pbuf, psend, fbuf, gbuf, fsend, onehot, slotmask, zrest, zfirst, geo, back, spread, gdense, halves,
    w_in_half, w_mix_half, w_ve, w_ve_t, w_mix_t, w_two_t, w_in_t, w_hid_rows, w_out_col, same2,
    same16, seg,
    pos_ref, vel_ref, kind_ref, nbr_ref, emb_ref, w_in_ref, w_two_ref, w_val_ref, w_env_ref,
    w_mix_ref, w_lat_ref, w_out_ref,
    pos_sems, frc_sems, own_sems, load_sems,
):
    loads = [
        pltpu.make_async_copy(src, dst, load_sems.at[i])
        for i, (src, dst) in enumerate(
            (
                (pos_hbm, pos_ref), (vel_hbm, vel_ref), (kind_hbm, kind_ref), (nbr_hbm, nbr_ref),
                (emb_hbm, emb_ref), (w_in_hbm, w_in_ref), (w_two_hbm, w_two_ref),
                (w_val_hbm, w_val_ref), (w_env_hbm, w_env_ref), (w_mix_hbm, w_mix_ref),
                (w_lat_hbm, w_lat_ref), (w_out_hbm, w_out_ref),
            )
        )
    ]
    for load in loads:
        load.start()
    mx, my = lax.axis_index("dx"), lax.axis_index("dy")
    near = [(p, q) for p in (-1, 0, 1) for q in (-1, 0, 1) if (p, q) != (0, 0)]
    wide_area = [
        (p, q) for p in range(-2, 3) for q in range(-2, 3) if (p, q) != (0, 0)
    ]

    def device(p, q):
        return (lax.rem(mx + (p + nx), nx), lax.rem(my + (q + ny), ny))

    barrier = pltpu.get_barrier_semaphore()
    for p, q in wide_area:
        pl.semaphore_signal(barrier, inc=1, device_id=device(p, q), device_id_type=MESH)

    def pos_copy(p, q):
        here, there = 3 * (p + 1) + q + 1, 3 * (1 - p) + 1 - q
        return pltpu.make_async_remote_copy(
            src_ref=psend, dst_ref=pbuf.at[there],
            send_sem=pos_sems.at[0, here], recv_sem=pos_sems.at[1, there],
            device_id=device(p, q), device_id_type=MESH,
        )

    def frc_copy(t, p, q):
        here, there = 5 * (p + 2) + q + 2, 5 * (2 - p) + 2 - q

        def box(ref, dp, dq):
            low_p, low_q = max(-1, p - 1), max(-1, q - 1)
            return ref.at[
                pl.ds(low_p - dp + 1, 3 - abs(p)), pl.ds(low_q - dq + 1, 3 - abs(q))
            ]

        return pltpu.make_async_remote_copy(
            src_ref=box(fsend.at[t], 0, 0), dst_ref=box(gbuf.at[t, there], p, q),
            send_sem=frc_sems.at[0, t, here], recv_sem=frc_sems.at[1, t, there],
            device_id=device(p, q), device_id_type=MESH,
        )

    def own_copy(p, q):
        here, there = 3 * (p + 1) + q + 1, 3 * (1 - p) + 1 - q
        return pltpu.make_async_remote_copy(
            src_ref=fsend.at[STEPS, p + 1, q + 1], dst_ref=fbuf.at[there],
            send_sem=own_sems.at[0, here], recv_sem=own_sems.at[1, there],
            device_id=device(p, q), device_id_type=MESH,
        )

    for load in loads[0:3]:
        load.wait()
    kinds = kind_ref[0].astype(F32)
    start = jnp.concatenate(
        [pos_ref[0, :, 0, :], kinds, vel_ref[0, :, 0, :], jnp.zeros((1, LANES), F32)], axis=0
    )
    psend[...] = start
    pl.semaphore_wait(barrier, len(wide_area))
    for p, q in near:
        pos_copy(p, q).start()

    pbuf[4] = start
    fsend[...] = jnp.zeros(fsend.shape, F32)

    def inv_mass(kind):
        mass = jnp.zeros((1, LANES), F32)
        for k in range(NS):
            mass = mass + jnp.where(kind == float(k), MASSES[k], 0.0)
        return 1.0 / mass

    for load in loads[3:]:
        load.wait()
    val_t, env_t = w_val_ref[...].astype(F32), w_env_ref[...].astype(F32)
    w_ve[0 : 3 * C, :] = val_t.T.astype(BF16)
    w_ve[3 * C : 6 * C, :] = env_t.T.astype(BF16)
    w_ve_t[...] = jnp.concatenate([val_t, env_t], axis=1).astype(BF16)
    w_in_half[...] = (0.5 * w_in_ref[...].astype(F32).T).astype(BF16)
    w_mix_half[...] = (0.5 * w_mix_ref[...].astype(F32)).astype(BF16)
    w_two_t[...] = (0.5 * w_two_ref[...].astype(F32).T).astype(BF16)
    w_in_t[...] = w_in_ref[0:16]
    out_col = column(w_out_ref[...].reshape(1, C), C)
    w_out_col[...] = out_col
    w_hid = jnp.sum(w_lat_ref[...].astype(F32) * out_col, axis=0, keepdims=True)
    w_hid_col = column(w_hid, HID)
    w_mix_t[...] = (
        (0.5 * w_mix_ref[...].astype(F32)) * jnp.concatenate([w_hid_col] * 2, axis=1)
    ).T.astype(BF16)
    hid_hi = w_hid.astype(BF16).astype(F32)
    row16 = iota((16, LANES), 0)
    w_hid_rows[...] = jnp.where(
        row16 == 0, hid_hi, jnp.where(row16 == 1, w_hid - hid_hi, 0.0)
    ).astype(BF16)
    lane_r, lane_c = iota((LANES, LANES), 0), iota((LANES, LANES), 1)
    together = jnp.where(lane_r // SLOTS == lane_c // SLOTS, 1.0 / SLOTS, 0.0)
    same16[...] = together.astype(BF16)
    pair_r, pair_c = iota((2 * LANES, 2 * LANES), 0), iota((2 * LANES, 2 * LANES), 1)
    same2[...] = jnp.where(pair_r // SLOTS == pair_c // SLOTS, 1.0 / SLOTS, 0.0).astype(BF16)
    seg[...] = jnp.where(lane_r // SLOTS == lane_c % CENTERS, 1.0, 0.0).astype(BF16)

    nbrs = nbr_ref[0, 0]
    valid = jnp.where(nbrs >= 0, 1.0, 0.0)
    index = jnp.maximum(nbrs, 0)
    atom = jnp.bitwise_and(index, LANES - 1)
    slot = jnp.right_shift(index, 7)
    gdense[0] = atom.astype(F32)
    gdense[1] = slot.astype(F32)
    row_b, lane_b = iota((NB, LANES), 0), iota((NB, LANES), 1)
    centre_index = row_b * CENTERS + lane_b // SLOTS
    owner = jnp.where(lane_b // CENTERS == row_b, 1.0, 0.0)
    slot_x = (slot // 3).astype(F32) - 1.0
    slot_y = jnp.remainder(slot, 3).astype(F32) - 1.0

    def one_hots(i, carry):
        for j in range(2):
            b = 2 * i + j
            onehot[i, :, j * LANES : (j + 1) * LANES] = jnp.where(
                lane_r.astype(F32) == gdense[0, pl.ds(b, 1), :], 1.0, 0.0
            ).astype(BF16)
            slotmask[b] = jnp.where(row16.astype(F32) == gdense[1, pl.ds(b, 1), :], 1.0, 0.0)
        return carry

    lax.fori_loop(0, NB // 2, one_hots, 0)

    row8 = iota((8, LANES), 0)
    emb_t = emb_ref[...].astype(F32).T
    blank = jnp.zeros((EMB, NS), F32)
    emb_both = jnp.concatenate(
        [jnp.concatenate([emb_t, blank], axis=1), jnp.concatenate([blank, emb_t], axis=1)], axis=0
    ).astype(BF16)

    for p, q in near:
        pos_copy(p, q).wait_recv()
    far_kind = jnp.zeros((NB, LANES), F32)
    for o in range(9):
        far_kind = jnp.where(slot == o, lane_pick(pbuf[o, 3:4, :], atom), far_kind)
    for o in range(9):
        halves[o] = jnp.broadcast_to(
            (0.5 * TIME_STEP) * inv_mass(pbuf[o, 3:4, :]), (8, LANES)
        )
    gdense[0] = lane_pick(kinds, centre_index)
    gdense[1] = far_kind
    kind_of = jnp.where(row8 < NS, row8, row8 - NS).astype(F32)
    chosen = jnp.concatenate(
        [
            jnp.where(
                kind_of == jnp.where(row8 < NS, gdense[0, b : b + 1, :], gdense[1, b : b + 1, :]),
                1.0, 0.0,
            ).astype(BF16)
            for b in range(NB)
        ],
        axis=1,
    )
    looked = dot(emb_both, chosen)
    for b in range(NB):
        zfirst[b] = looked[0:8, b * LANES : (b + 1) * LANES]
        zrest[b] = looked[8 : 2 * EMB, b * LANES : (b + 1) * LANES].astype(BF16)

    slot_lane = lane_b // SLOTS * SLOTS + row_b
    lane_atom = lane_b // SLOTS

    def wide(parts):
        return jnp.concatenate(parts, axis=1)

    def tall(parts):
        return jnp.concatenate(parts, axis=0)

    def part(x, j):
        return x[:, j * LANES : (j + 1) * LANES]

    def order(x, l):
        return x[l * C : (l + 1) * C]

    def corner(a, b):
        zero = jnp.zeros((LANES, LANES), BF16)
        return tall([wide([a, zero]), wide([zero, b])])

    def chain(tiles):
        count = len(tiles)
        each = range(count)

        def gather(values):
            return [[] for _ in range(values)]

        def mix_slots(x, gram):
            first = dot(tall([order(x[i], 0) for i in each]), same2[...]).astype(BF16)
            yield None
            mixed = []
            for i in each:
                mixed.append(
                    tall(
                        [order(first, i)]
                        + [dot(order(x[i], l), gram[i][l - 1]).astype(BF16) for l in (1, 2)]
                    )
                )
                yield None
            yield mixed

        cut, cut16, a1, hidden, slope1, pre, latent16, value, envw, a2, hidden2, slope2 = gather(12)
        d_a2, readout, d_mixed, d_value, d_envat, d_latent, d_hidden, picks, gram = gather(9)
        for i in each:
            pair = (2 * tiles[i], 2 * tiles[i] + 1)
            cut.append(wide([geo[b, 16:17, :] for b in pair]))
            cut16.append(cut[i].astype(BF16))
            top = wide([tall([geo[b, 0:8, :], zfirst[b]]) for b in pair])
            zin = tall([top.astype(BF16), wide([zrest[b] for b in pair])])
            a1.append(dot(w_in_half[...], zin))
            yield
        for i in each:
            act, slope = gate(a1[i])
            hidden.append(act)
            slope1.append(slope)
            yield
        for i in each:
            pre.append(dot(w_two_ref[...], hidden[i]))
            latent16.append((pre[i] * cut[i]).astype(BF16))
            yield
        for i in each:
            blockwise = []
            for b in (2 * tiles[i], 2 * tiles[i] + 1):
                sph = geo[b, 8:16, :]
                rows = [sph[m : m + 1] for m in range(8)]
                far = [lane_pick(row, slot_lane) for row in rows]
                terms = [far[m] * rows[m] for m in range(8)]
                compact = [
                    (terms[0] + terms[1]) + terms[2],
                    ((terms[3] + terms[4]) + (terms[5] + terms[6])) + terms[7],
                ]
                picks.append(far)
                blockwise.append([tall([x.astype(BF16)] * CENTERS) * same16[...] for x in compact])
            gram.append([corner(blockwise[0][l], blockwise[1][l]) for l in range(2)])
            yield
        for i in each:
            value_envw = dot(w_ve[...], latent16[i])
            value.append(value_envw[0 : 3 * C].astype(BF16))
            envw.append(value_envw[3 * C : 6 * C].astype(BF16))
            yield
        for env_at in mix_slots(envw, gram):
            if env_at is None:
                yield
        for i in each:
            mixed = tall([latent16[i], value[i] * env_at[i]])
            a2.append(dot(w_mix_half[...], mixed))
            yield
        for i in each:
            act, slope = gate(a2[i])
            hidden2.append(act)
            d_a2.append(slope * cut16[i])
            yield
        for i in each:
            d_mixed.append(dot(w_mix_t[...], d_a2[i]))
            d_scal = d_mixed[i][C : 4 * C].astype(BF16)
            d_value.append(d_scal * env_at[i])
            d_envat.append(d_scal * value[i])
            yield
        for i in each:
            for j in range(2):
                dq, ew = part(d_envat[i], j), part(envw[i], j)
                left = tall([order(dq, 1), order(ew, 1), order(dq, 2), order(ew, 2)])
                right = corner(
                    tall([order(ew, 1), order(dq, 1)]), tall([order(ew, 2), order(dq, 2)])
                )
                pair = lax.dot_general(
                    left, right, (((0,), (0,)), ((), ())), preferred_element_type=F32
                )
                sums = []
                for l in range(2):
                    full = part(pair, l)
                    own = full[0:SLOTS]
                    for a in range(1, CENTERS):
                        own = jnp.where(
                            lane_atom == a, full[a * SLOTS : (a + 1) * SLOTS], own
                        )
                    sums.append(own)
                for m in range(8):
                    product = sums[0 if m < 3 else 1] * picks[2 * i + j][m]
                    spread[m, 2 * tiles[i] + j] = product[0:8] + product[8:16]
                yield
        for d_envw in mix_slots(d_envat, gram):
            if d_envw is None:
                yield
        for i in each:
            both = dot(w_hid_rows[...], hidden2[i])
            readout.append(both[0:1] + both[1:2])
            energy_part = wide([w_out_col[...]] * 2) * cut[i]
            rest = dot(w_ve_t[...], tall([d_value[i], d_envw[i]]))
            d_latent.append((d_mixed[i][0:C] + rest) + energy_part)
            d_cut = readout[i] + jnp.sum(
                pre[i] * (d_latent[i] + energy_part), axis=0, keepdims=True
            )
            for j in range(2):
                back[2 * tiles[i] + j, 8:9, :] = part(d_cut, j)
            yield
        for i in each:
            d_hidden.append(dot(w_two_t[...], (d_latent[i] * cut[i]).astype(BF16)).astype(BF16))
            yield
        for i in each:
            d_basis = dot(w_in_t[...], d_hidden[i] * slope1[i])
            for j in range(2):
                back[2 * tiles[i] + j, 0:8, :] = part(d_basis, j)[0:8]
            yield

    def run_chains(lag):
        waiting = [chain(list(range(i, i + GB // 2))) for i in range(0, NB // 2, GB // 2)]
        running = []
        step = 0
        while waiting or running:
            while waiting and (lag == 0 or step % lag == 0):
                running.append(waiting.pop(0))
                if lag:
                    break
            for one in list(running):
                if next(one, 0) == 0:
                    running.remove(one)
            step += 1

    far_first = sorted(wide_area, key=lambda o: (abs(o[0]) + abs(o[1]), o))
    middle = iota((3, LANES), 0) == 1

    def evaluate(t, carry):
        here = pbuf[4]
        rel = []
        for k in range(3):
            far = jnp.zeros((NB, LANES), F32)
            for o in range(9):
                far = jnp.where(slot == o, lane_pick(pbuf[o, k : k + 1, :], atom), far)
            if k == 0:
                far = far + slot_x
            if k == 1:
                far = far + slot_y
            rel.append(far - lane_pick(here[k : k + 1], centre_index))
        dist_sq = rel[0] * rel[0] + rel[1] * rel[1] + rel[2] * rel[2] + SOFTEN
        dist = jnp.sqrt(dist_sq)
        inv = 1.0 / dist
        ux, uy, uz = rel[0] * inv, rel[1] * inv, rel[2] * inv
        fall = 1.0 - dist_sq * (1.0 / (CUTOFF * CUTOFF))
        cut = valid * fall * fall
        theta = dist * (math.pi / CUTOFF)
        sin1, cos1 = jnp.sin(theta), jnp.cos(theta)
        sines, cosines = [sin1], [cos1]
        for n in range(1, NBASIS):
            s, c = sines[-1], cosines[-1]
            sines.append(s * cos1 + c * sin1)
            cosines.append(c * cos1 - s * sin1)
        for n in range(NBASIS):
            geo[:, n, :] = sines[n] * inv * cut
        sph = (
            R3 * ux, R3 * uy, R3 * uz, R15 * ux * uy, R15 * uy * uz,
            0.5 * R5 * (3.0 * uz * uz - 1.0), R15 * ux * uz, 0.5 * R15 * (ux * ux - uy * uy),
        )
        for m in range(8):
            geo[:, 8 + m, :] = sph[m]
        geo[:, 16, :] = cut

        run_chains(LAG)

        d_sph = []
        for m in range(8):
            parts = [spread[m, :, i, :] for i in range(8)]
            total = ((parts[0] + parts[1]) + (parts[2] + parts[3])) + (
                (parts[4] + parts[5]) + (parts[6] + parts[7])
            )
            d_sph.append(total * (1.0 / SLOTS))
        d1, d2, d3, d4, d5, d6, d7, d8 = d_sph
        du = (
            R3 * d1 + R15 * (uy * d4 + uz * d7 + ux * d8),
            R3 * d2 + R15 * (ux * d4 + uz * d5 - uy * d8),
            R3 * d3 + R15 * (uy * d5 + ux * d7) + (3.0 * R5) * (uz * d6),
        )
        by_sin = jnp.zeros((NB, LANES), F32)
        by_cos = jnp.zeros((NB, LANES), F32)
        for n in range(NBASIS):
            d_basis = back[:, n, :]
            by_sin = by_sin + d_basis * sines[n]
            by_cos = by_cos + (d_basis * cosines[n]) * ((n + 1) * math.pi / CUTOFF)
        by_sin = by_sin * inv
        d_cut = back[:, 8, :] + by_sin
        d_dist = cut * inv * (by_cos - by_sin) - inv * (du[0] * ux + du[1] * uy + du[2] * uz)
        d_sq = 0.5 * inv * d_dist - d_cut * (valid * fall) * (2.0 / (CUTOFF * CUTOFF))
        grads = [(du[k] * inv + 2.0 * rel[k] * d_sq) * valid for k in range(3)]

        split = []
        for k in range(3):
            high = grads[k].astype(BF16).astype(F32)
            gdense[k] = high
            gdense[3 + k] = grads[k] - high
        segs = dot(gdense[...].reshape(6 * NB, LANES).astype(BF16), seg[...])
        centre = [
            jnp.sum(
                (segs[k * NB : (k + 1) * NB] + segs[(3 + k) * NB : (4 + k) * NB]) * owner,
                axis=0, keepdims=True,
            )
            for k in range(3)
        ]
        sums = [jnp.zeros((6 * 16, LANES), F32)] * 2
        for i in range(NB // 2):
            left = wide(
                [
                    tall([gdense[k, b : b + 1, :] * slotmask[b] for k in range(6)]).astype(BF16)
                    for b in (2 * i, 2 * i + 1)
                ]
            )
            sums[i % 2] = sums[i % 2] + lax.dot_general(
                left, onehot[i], (((1,), (1,)), ((), ())), preferred_element_type=F32
            )
        scattered = sums[0] + sums[1]
        ghost = [
            scattered[k * 16 : (k + 1) * 16] + scattered[(3 + k) * 16 : (4 + k) * 16]
            for k in range(3)
        ]
        for k in range(3):
            for p in range(3):
                terms = -ghost[k][3 * p : 3 * p + 3]
                if p == 1:
                    terms = terms + jnp.where(middle, centre[k], 0.0)
                fsend[t, p, :, k, :] = terms

        @pl.when(t < STEPS)
        def _():
            for p, q in reversed(far_first):
                frc_copy(t, p, q).start()
            for p, q in far_first:
                frc_copy(t, p, q).wait_recv()
            for dp in range(-1, 2):
                for dq in range(-1, 2):
                    force = fsend[t, dp + 1, dq + 1]
                    for a in range(dp - 1, dp + 2):
                        for b in range(dq - 1, dq + 2):
                            if (a, b) != (0, 0):
                                force = force + gbuf[t, 5 * (a + 2) + b + 2, dp + 1, dq + 1]
                    slot_at = 3 * (dp + 1) + dq + 1
                    kick = halves[slot_at, 0:1, :] * force[0:3]
                    speed = pbuf[slot_at, 4:7, :]
                    speed = speed + jnp.where(t > 0, 1.0, 0.0) * kick
                    speed = speed + kick
                    pbuf[slot_at, 4:7, :] = speed
                    pbuf[slot_at, 0:3, :] = pbuf[slot_at, 0:3, :] + TIME_STEP * speed
            for p, q in far_first:
                frc_copy(t, p, q).wait_send()

        return carry

    lax.fori_loop(0, EVALS, evaluate, 0)
    for p, q in near:
        own_copy(p, q).start()
    for p, q in near:
        pos_copy(p, q).wait_send()
    for p, q in near:
        own_copy(p, q).wait_recv()
    force = fsend[STEPS, 1, 1]
    for p, q in near:
        force = force + fbuf[3 * (p + 1) + q + 1]
    speed = pbuf[4, 4:7, :] + halves[4, 0:1, :] * force[0:3]
    pos_out[0, :, 0, :] = pbuf[4, 0:3, :]
    vel_out[0, :, 0, :] = speed
    frc_out[0, :, 0, :] = force[0:3]
    for p, q in near:
        own_copy(p, q).wait_send()


def solution(mesh):
    nx, ny = mesh.shape["dx"], mesh.shape["dy"]

    def per_device(positions, velocities, species, neighbours, emb, w_in, w_two, w_val, w_env, *more):
        rows = (0, 2, 1, 3)
        args = (
            positions.transpose(rows), velocities.transpose(rows), species, neighbours, emb,
            w_in.T, w_two, w_val.T, w_env.T, *more,
        )

        def body(*refs):
            kernel(nx, ny, *refs)

        vmem = pl.BlockSpec(memory_space=pltpu.VMEM)
        out = jax.ShapeDtypeStruct((1, 3, 1, LANES), F32)
        results = pl.pallas_call(
            body,
            out_shape=(out, out, out),
            in_specs=[pl.BlockSpec(memory_space=pltpu.HBM)] * len(args),
            out_specs=(vmem, vmem, vmem),
            scratch_shapes=[
                pltpu.VMEM((9, 8, LANES), F32),
                pltpu.VMEM((8, LANES), F32),
                pltpu.VMEM((9, 4, LANES), F32),
                pltpu.VMEM((STEPS, 25, 3, 3, 4, LANES), F32),
                pltpu.VMEM((EVALS, 3, 3, 4, LANES), F32),
                pltpu.VMEM((NB // 2, LANES, 2 * LANES), BF16),
                pltpu.VMEM((NB, 16, LANES), F32),
                pltpu.VMEM((NB, 48, LANES), BF16),
                pltpu.VMEM((NB, 8, LANES), F32),
                pltpu.VMEM((NB, 24, LANES), F32),
                pltpu.VMEM((NB, 16, LANES), F32),
                pltpu.VMEM((8, NB, 8, LANES), F32),
                pltpu.VMEM((6, NB, LANES), F32),
                pltpu.VMEM((9, 8, LANES), F32),
                pltpu.VMEM((HID, NBASIS + 2 * EMB), BF16),
                pltpu.VMEM((HID, 4 * C), BF16),
                pltpu.VMEM((6 * C, C), BF16),
                pltpu.VMEM((C, 6 * C), BF16),
                pltpu.VMEM((4 * C, HID), BF16),
                pltpu.VMEM((HID, C), BF16),
                pltpu.VMEM((16, HID), BF16),
                pltpu.VMEM((16, HID), BF16),
                pltpu.VMEM((C, LANES), F32),
                pltpu.VMEM((2 * LANES, 2 * LANES), BF16),
                pltpu.VMEM((LANES, LANES), BF16),
                pltpu.VMEM((LANES, LANES), BF16),
                *[pltpu.VMEM(x.shape, x.dtype) for x in args],
                pltpu.SemaphoreType.DMA((2, 9)),
                pltpu.SemaphoreType.DMA((2, STEPS, 25)),
                pltpu.SemaphoreType.DMA((2, 9)),
                pltpu.SemaphoreType.DMA((len(args),)),
            ],
            compiler_params=pltpu.CompilerParams(
                collective_id=0, has_side_effects=True, vmem_limit_bytes=VMEM_BYTES
            ),
        )(*args)

        def hand_over(*refs):
            sems = refs[6]
            copies = [
                pltpu.make_async_copy(refs[i], refs[3 + i], sems.at[i]) for i in range(3)
            ]
            for copy in copies:
                copy.start()
            for copy in copies:
                copy.wait()

        hbm = pl.BlockSpec(memory_space=pltpu.HBM)
        results = pl.pallas_call(
            hand_over,
            out_shape=(out, out, out),
            in_specs=[hbm] * 3,
            out_specs=(hbm, hbm, hbm),
            scratch_shapes=[pltpu.SemaphoreType.DMA((3,))],
            compiler_params=pltpu.CompilerParams(vmem_limit_bytes=VMEM_BYTES),
        )(*results)
        return tuple(x.transpose(rows) for x in results)

    grid4 = P("dx", "dy", None, None)
    in_specs = (grid4, grid4, P("dx", "dy", None), grid4) + (P(),) * 8
    return jax.shard_map(
        per_device, mesh=mesh, in_specs=in_specs, out_specs=(grid4, grid4, grid4), check_vma=False
    )
```

time: 74.3 us -> 48.5 us (0.65)
  Pallas kernels: 68.6 us -> 47.8 us
  local copies, waits for them, and re-layouts: 4.71 us -> 0 us
    pallas_call x1 -> x2, Pallas kernels: 68.6 us -> 47.8 us  [the longest x1 46.5 us: per_device(): pl.pallas_call(body, out_shape=(out, out, out), in_specs=[pl.BlockSpec(me...]
    unnamed x23 -> x0, local copies, waits for them, and re-layouts: 3.02 us -> none
    pallas_call x3 -> x0, local copies, waits for them, and re-layouts: 1.69 us -> none  [per_device(): pl.pallas_call(body, out_shape=(out, out, out), in_specs=[vmem] * len(arg...]
where the time goes in v2:
time: 48.5 us; the launch traced here: 48.4 us
  Pallas kernels  47.8 us (99%)
  between operations  0.64 us (1%)
    pallas_call x1, Pallas kernels, per_device(): pl.pallas_call(body, out_shape=(out, out, out), in_specs=[pl.BlockSpec(me...  46.5 us
    pallas_call x1, Pallas kernels, per_device(): pl.pallas_call(hand_over, out_shape=(out, out, out), in_specs=[hbm] * 3,...  1.27 us

profile of v2, /device:TPU:1, one launch (start us, length us, event | category | flops | bytes accessed | tf_op | source)
XLA Modules:
  0.0 48.4 jit_solution(14021116251541814870)
XLA Ops:
  0.6 46.5 %shard_map.139 = (f32[1,3,1,128]{3,2,1,0:T(1,128)}, f32[1,3,1,128]{3,2,1,0:T(1,128)}, f32[1,3,1,128]{3,2,1,0:T(1,128)}) custom-call(f32[1,3,1,128]{3,2,1,0:T(1,128)} %bitcast.17, f32[1,3,1,128]{3,2,1,0:T(1,128)} %bitcast.18, s32[1,1,128]{2,1,0:T(1,128)} %refs_2_.1, s32[1,1,16,128]{3,2,1,0:T(8,128)} %refs_3_.1, bf16[4,28]{1,0:T(4,128)(2,1)} %refs_4_.1, ...), custom_call_target="tpu_custom_call" | custom-call | tf_op jit(solution)/shard_map/pallas_call | solution.py:560
  47.2 1.3 %shard_map.140 = (f32[1,3,1,128]{3,2,1,0:T(1,128)}, f32[1,3,1,128]{3,2,1,0:T(1,128)}, f32[1,3,1,128]{3,2,1,0:T(1,128)}) custom-call(f32[1,3,1,128]{3,2,1,0:T(1,128)} %get-tuple-element.9.refs_0_, f32[1,3,1,128]{3,2,1,0:T(1,128)} %get-tuple-element.10.refs_1_, f32[1,3,1,128]{3,2,1,0:T(1,128)} %get-tuple-element.11.refs_2_), custom_call_target="tpu_custom_call" | custom-call | tf_op jit(solution)/shard_map/pallas_call | solution.py:614

commit v3 on v2

--- a/solution.py
+++ b/solution.py
@@ -69,7 +69,7 @@
     pos_hbm, vel_hbm, kind_hbm, nbr_hbm, emb_hbm, w_in_hbm, w_two_hbm, w_val_hbm, w_env_hbm,
     w_mix_hbm, w_lat_hbm, w_out_hbm,
     pos_out, vel_out, frc_out,
-    pbuf, psend, fbuf, gbuf, fsend, onehot, slotmask, zrest, zfirst, geo, back, spread, gdense, halves,
+    pbuf, psend, fbuf, gbuf, fsend, onehot, slotmask, zrest, zfirst, geo, back, adder, gdense, halves,
     w_in_half, w_mix_half, w_ve, w_ve_t, w_mix_t, w_two_t, w_in_t, w_hid_rows, w_out_col, same2,
     same16, seg,
     pos_ref, vel_ref, kind_ref, nbr_ref, emb_ref, w_in_ref, w_two_ref, w_val_ref, w_env_ref,
@@ -87,8 +87,6 @@
             )
         )
     ]
-    for load in loads:
-        load.start()
     mx, my = lax.axis_index("dx"), lax.axis_index("dy")
     near = [(p, q) for p in (-1, 0, 1) for q in (-1, 0, 1) if (p, q) != (0, 0)]
     wide_area = [
@@ -99,8 +97,13 @@
         return (lax.rem(mx + (p + nx), nx), lax.rem(my + (q + ny), ny))
 
     barrier = pltpu.get_barrier_semaphore()
-    for p, q in wide_area:
+    near_last = sorted(near, key=lambda o: -abs(o[0]) - abs(o[1]))
+    far_first = sorted(wide_area, key=lambda o: (-abs(o[0]) - abs(o[1]), o))
+    for p, q in near_last:
         pl.semaphore_signal(barrier, inc=1, device_id=device(p, q), device_id_type=MESH)
+
+    for load in loads:
+        load.start()
 
     def pos_copy(p, q):
         here, there = 3 * (p + 1) + q + 1, 3 * (1 - p) + 1 - q
@@ -140,8 +143,8 @@
         [pos_ref[0, :, 0, :], kinds, vel_ref[0, :, 0, :], jnp.zeros((1, LANES), F32)], axis=0
     )
     psend[...] = start
-    pl.semaphore_wait(barrier, len(wide_area))
-    for p, q in near:
+    pl.semaphore_wait(barrier, len(near))
+    for p, q in near_last:
         pos_copy(p, q).start()
 
     pbuf[4] = start
@@ -180,6 +183,9 @@
     same16[...] = together.astype(BF16)
     pair_r, pair_c = iota((2 * LANES, 2 * LANES), 0), iota((2 * LANES, 2 * LANES), 1)
     same2[...] = jnp.where(pair_r // SLOTS == pair_c // SLOTS, 1.0 / SLOTS, 0.0).astype(BF16)
+    adder[...] = jnp.where(
+        iota((16, C), 0) == iota((16, C), 1) // 8, 1.0 / SLOTS, 0.0
+    ).astype(BF16)
     seg[...] = jnp.where(lane_r // SLOTS == lane_c % CENTERS, 1.0, 0.0).astype(BF16)
 
     nbrs = nbr_ref[0, 0]
@@ -337,6 +343,25 @@
             d_value.append(d_scal * env_at[i])
             d_envat.append(d_scal * value[i])
             yield
+        for d_envw in mix_slots(d_envat, gram):
+            if d_envw is None:
+                yield
+        for i in each:
+            both = dot(w_hid_rows[...], hidden2[i])
+            readout.append(both[0:1] + both[1:2])
+            energy_part = wide([w_out_col[...]] * 2) * cut[i]
+            rest = dot(w_ve_t[...], tall([d_value[i], d_envw[i]]))
+            d_latent.append((d_mixed[i][0:C] + rest) + energy_part)
+            d_cut = readout[i] + jnp.sum(
+                pre[i] * (d_latent[i] + energy_part), axis=0, keepdims=True
+            )
+            for j in range(2):
+                back[2 * tiles[i] + j, 16:17, :] = part(d_cut, j)
+            yield
+        for i in each:
+            d_hidden.append(dot(w_two_t[...], (d_latent[i] * cut[i]).astype(BF16)).astype(BF16))
+            yield
+        stacks = []
         for i in each:
             for j in range(2):
                 dq, ew = part(d_envat[i], j), part(envw[i], j)
@@ -356,32 +381,21 @@
                             lane_atom == a, full[a * SLOTS : (a + 1) * SLOTS], own
                         )
                     sums.append(own)
+                stack = []
                 for m in range(8):
                     product = sums[0 if m < 3 else 1] * picks[2 * i + j][m]
-                    spread[m, 2 * tiles[i] + j] = product[0:8] + product[8:16]
+                    stack.append(product[0:8] + product[8:16])
+                stacks.append(tall(stack).astype(BF16))
                 yield
-        for d_envw in mix_slots(d_envat, gram):
-            if d_envw is None:
-                yield
-        for i in each:
-            both = dot(w_hid_rows[...], hidden2[i])
-            readout.append(both[0:1] + both[1:2])
-            energy_part = wide([w_out_col[...]] * 2) * cut[i]
-            rest = dot(w_ve_t[...], tall([d_value[i], d_envw[i]]))
-            d_latent.append((d_mixed[i][0:C] + rest) + energy_part)
-            d_cut = readout[i] + jnp.sum(
-                pre[i] * (d_latent[i] + energy_part), axis=0, keepdims=True
-            )
-            for j in range(2):
-                back[2 * tiles[i] + j, 8:9, :] = part(d_cut, j)
-            yield
-        for i in each:
-            d_hidden.append(dot(w_two_t[...], (d_latent[i] * cut[i]).astype(BF16)).astype(BF16))
-            yield
         for i in each:
             d_basis = dot(w_in_t[...], d_hidden[i] * slope1[i])
             for j in range(2):
                 back[2 * tiles[i] + j, 0:8, :] = part(d_basis, j)[0:8]
+            yield
+        for i in each:
+            d_sph = dot(adder[...], wide(stacks[2 * i : 2 * i + 2]))
+            for j in range(2):
+                back[2 * tiles[i] + j, 8:16, :] = part(d_sph, j)[0:8]
             yield
 
     def run_chains(lag):
@@ -398,7 +412,6 @@
                     running.remove(one)
             step += 1
 
-    far_first = sorted(wide_area, key=lambda o: (abs(o[0]) + abs(o[1]), o))
     middle = iota((3, LANES), 0) == 1
 
     def evaluate(t, carry):
@@ -438,14 +451,7 @@
 
         run_chains(LAG)
 
-        d_sph = []
-        for m in range(8):
-            parts = [spread[m, :, i, :] for i in range(8)]
-            total = ((parts[0] + parts[1]) + (parts[2] + parts[3])) + (
-                (parts[4] + parts[5]) + (parts[6] + parts[7])
-            )
-            d_sph.append(total * (1.0 / SLOTS))
-        d1, d2, d3, d4, d5, d6, d7, d8 = d_sph
+        d1, d2, d3, d4, d5, d6, d7, d8 = [back[:, 8 + m, :] for m in range(8)]
         du = (
             R3 * d1 + R15 * (uy * d4 + uz * d7 + ux * d8),
             R3 * d2 + R15 * (ux * d4 + uz * d5 - uy * d8),
@@ -458,7 +464,7 @@
             by_sin = by_sin + d_basis * sines[n]
             by_cos = by_cos + (d_basis * cosines[n]) * ((n + 1) * math.pi / CUTOFF)
         by_sin = by_sin * inv
-        d_cut = back[:, 8, :] + by_sin
+        d_cut = back[:, 16, :] + by_sin
         d_dist = cut * inv * (by_cos - by_sin) - inv * (du[0] * ux + du[1] * uy + du[2] * uz)
         d_sq = 0.5 * inv * d_dist - d_cut * (valid * fall) * (2.0 / (CUTOFF * CUTOFF))
         grads = [(du[k] * inv + 2.0 * rel[k] * d_sq) * valid for k in range(3)]
@@ -501,9 +507,9 @@
 
         @pl.when(t < STEPS)
         def _():
+            for p, q in far_first:
+                frc_copy(t, p, q).start()
             for p, q in reversed(far_first):
-                frc_copy(t, p, q).start()
-            for p, q in far_first:
                 frc_copy(t, p, q).wait_recv()
             for dp in range(-1, 2):
                 for dq in range(-1, 2):
@@ -573,8 +579,8 @@
                 pltpu.VMEM((NB, 48, LANES), BF16),
                 pltpu.VMEM((NB, 8, LANES), F32),
                 pltpu.VMEM((NB, 24, LANES), F32),
-                pltpu.VMEM((NB, 16, LANES), F32),
-                pltpu.VMEM((8, NB, 8, LANES), F32),
+                pltpu.VMEM((NB, 24, LANES), F32),
+                pltpu.VMEM((16, C), BF16),
                 pltpu.VMEM((6, NB, LANES), F32),
                 pltpu.VMEM((9, 8, LANES), F32),
                 pltpu.VMEM((HID, NBASIS + 2 * EMB), BF16),

time: 48.5 us -> 47.3 us (0.975)
  Pallas kernels: 47.8 us -> 46.6 us
    pallas_call x1, Pallas kernels: 46.5 us -> 45.3 us  [per_device(): pl.pallas_call(body, out_shape=(out, out, out), in_specs=[pl.BlockSpec(me...]
where the time goes in v3:
time: 47.3 us; the launch traced here: 47.2 us
  Pallas kernels  46.6 us (99%)
  between operations  0.64 us (1%)
    pallas_call x1, Pallas kernels, per_device(): pl.pallas_call(body, out_shape=(out, out, out), in_specs=[pl.BlockSpec(me...  45.3 us
    pallas_call x1, Pallas kernels, per_device(): pl.pallas_call(hand_over, out_shape=(out, out, out), in_specs=[hbm] * 3,...  1.27 us

profile of v3, /device:TPU:1, one launch (start us, length us, event | category | flops | bytes accessed | tf_op | source)
XLA Modules:
  0.0 47.2 jit_solution(4800608272217554984)
XLA Ops:
  0.6 45.3 %shard_map.139 = (f32[1,3,1,128]{3,2,1,0:T(1,128)}, f32[1,3,1,128]{3,2,1,0:T(1,128)}, f32[1,3,1,128]{3,2,1,0:T(1,128)}) custom-call(f32[1,3,1,128]{3,2,1,0:T(1,128)} %bitcast.17, f32[1,3,1,128]{3,2,1,0:T(1,128)} %bitcast.18, s32[1,1,128]{2,1,0:T(1,128)} %refs_2_.1, s32[1,1,16,128]{3,2,1,0:T(8,128)} %refs_3_.1, bf16[4,28]{1,0:T(4,128)(2,1)} %refs_4_.1, ...), custom_call_target="tpu_custom_call" | custom-call | tf_op jit(solution)/shard_map/pallas_call | solution.py:566
  45.9 1.3 %shard_map.140 = (f32[1,3,1,128]{3,2,1,0:T(1,128)}, f32[1,3,1,128]{3,2,1,0:T(1,128)}, f32[1,3,1,128]{3,2,1,0:T(1,128)}) custom-call(f32[1,3,1,128]{3,2,1,0:T(1,128)} %get-tuple-element.9.refs_0_, f32[1,3,1,128]{3,2,1,0:T(1,128)} %get-tuple-element.10.refs_1_, f32[1,3,1,128]{3,2,1,0:T(1,128)} %get-tuple-element.11.refs_2_), custom_call_target="tpu_custom_call" | custom-call | tf_op jit(solution)/shard_map/pallas_call | solution.py:620
